TPU v7x, 32 devices: a whole 2x2x4 slice. The times are simulated.
32 devices in a mesh: groups: 2 (over y), tok: 4 (over z), tp: 2 (over x), sub: 2 (over core).
Axes of the slice: x: 2, y: 2, z: 4, core: 2. Of those that a mesh axis runs over, the one named last changes fastest.
Arguments:
- tokens: bfloat16 [4096, 8192], P(('groups', 'tok'), ('tp', 'sub')), parts along dimension 0, may hold values from -6 to 6
- frozen_key_weight: bfloat16 [8192, 1024], P(('tp', 'sub')), may hold values from -0.0625 to 0.0625
- output_gradient: bfloat16 [4096, 1024], P(('groups', 'tok'), ('tp', 'sub')), parts along dimension 0, may hold values from -6 to 6
- counts: int32 [8, 4], P('groups'), parts along dimension 0, may hold values from 1 to 509, as said below
- placement: int32 [8, 4], P('groups'), parts along dimension 0, may hold values from 0 to 15, as said below
- adapter_sequence: int32 [32], P('groups'), parts along dimension 0, may hold values from 0 to 15, as said below
- adapter_down: bfloat16 [32, 8192, 64], P(('groups', 'tok'), ('tp', 'sub')), parts along dimension 0, may hold values from -6 to 6
- adapter_up: bfloat16 [32, 1024, 64], P(('groups', 'tok'), ('tp', 'sub')), parts along dimension 0, may hold values from -6 to 6
- down_first_moment: float32 [32, 8192, 64], P(('groups', 'tok'), ('tp', 'sub')), parts along dimension 0, may hold values from -0.3 to 0.3
- down_second_moment: float32 [32, 8192, 64], P(('groups', 'tok'), ('tp', 'sub')), parts along dimension 0, may hold values from 0.0001 to 0.01
- down_average: float32 [32, 8192, 64], P(('groups', 'tok'), ('tp', 'sub')), parts along dimension 0, may hold values from -6 to 6
- up_first_moment: float32 [32, 1024, 64], P(('groups', 'tok'), ('tp', 'sub')), parts along dimension 0, may hold values from -0.3 to 0.3
- up_second_moment: float32 [32, 1024, 64], P(('groups', 'tok'), ('tp', 'sub')), parts along dimension 0, may hold values from 0.0001 to 0.01
- up_average: float32 [32, 1024, 64], P(('groups', 'tok'), ('tp', 'sub')), parts along dimension 0, may hold values from -6 to 6
Outputs:
- key_output: bfloat16 [4096, 1024], P(('groups', 'tok'), ('tp', 'sub')), parts along dimension 0
- input_gradient: bfloat16 [4096, 8192], P(('groups', 'tok'), ('tp', 'sub')), parts along dimension 0
- fresh_down: bfloat16 [32, 8192, 64], P(('groups', 'tok'), ('tp', 'sub')), parts along dimension 0
- fresh_up: bfloat16 [32, 1024, 64], P(('groups', 'tok'), ('tp', 'sub')), parts along dimension 0
- average_down_new: float32 [32, 8192, 64], P(('groups', 'tok'), ('tp', 'sub')), parts along dimension 0
- average_up_new: float32 [32, 1024, 64], P(('groups', 'tok'), ('tp', 'sub')), parts along dimension 0
There are 2 independent parts, one for each index of `groups`. A program takes and returns all parts, laid end to end along the dimension named above; an argument that names none is the same for every part. Nothing has to cross between parts.
Inputs may be any that keep to these rules, and one draw needn't show every extreme that they name: `adapter_sequence`: a permutation; the adapters at positions p with p // 4 = j are owned by index j of tok. The tenant placement[j, s] is owned by index (j + s) mod 4 of tok, so each row names one tenant of every owner. `counts`: each row sums to 512.
All inputs are finite; a program needn't handle non-finite values.
Results may differ from a plain program's by a relative error of at most 0.0034.
Values may be sent and summed in bfloat16 or wider, within the bound.
No kernel may reach another device: no remote copies, remote signals or barrier semaphores. Data moves between devices by JAX's collectives and lax.ppermute only.
A program may use at most 128 MiB of HBM per device.

v0:
```python
import functools

import jax
import jax.numpy as jnp
from jax import lax
from jax.experimental import pallas as pl
from jax.experimental.pallas import tpu as pltpu
from jax.sharding import PartitionSpec as P

MODEL_WIDTH = 8192
ADAPTER_RANK = 64

adapter_scale = 0.5
learn_rate = 0.3
beta_one = 0.9
beta_two = 0.99
adam_eps = 1e-08
ema_decay = 0.9

LOW_SCALE = MODEL_WIDTH ** (-0.5)
BACK_SCALE = ADAPTER_RANK ** (-0.5)
MIB = 1024 * 1024

f32 = jnp.float32
bf16 = jnp.bfloat16

SMEM = pl.BlockSpec(memory_space=pltpu.SMEM)
VMEM = pl.BlockSpec(memory_space=pltpu.VMEM)
ANY = pl.BlockSpec(memory_space=pl.ANY)
HBM = pl.BlockSpec(memory_space=pltpu.HBM)


def shape_of(shape, dtype):
    return jax.ShapeDtypeStruct(tuple(shape), dtype)


SCHEDULE_SCALE = 3


def cost(flops, bytes_accessed):
    return pl.CostEstimate(
        flops=int(flops * SCHEDULE_SCALE),
        bytes_accessed=int(bytes_accessed * SCHEDULE_SCALE),
        transcendentals=0,
    )


def params(mib):
    return pltpu.CompilerParams(vmem_limit_bytes=mib * MIB)


def nt(a, b):
    return lax.dot_general(a, b, (((1,), (1,)), ((), ())), preferred_element_type=f32)


def nn(a, b):
    return lax.dot_general(a, b, (((1,), (0,)), ((), ())), preferred_element_type=f32)


def tn(a, b):
    return lax.dot_general(a, b, (((0,), (0,)), ((), ())), preferred_element_type=f32)


def facts_kernel(slots, owned, tok_size, counts, placement, sequence, facts):
    me = lax.axis_index("tok")
    total = jnp.int32(0)
    for s in range(slots):
        total = total + counts[me, s]
        facts[s] = total
        tenant = placement[lax.rem(me - s + tok_size, tok_size), s]
        place = jnp.int32(0)
        for k in range(1, owned):
            place = place + jnp.where(sequence[me * owned + k] == tenant, k, 0)
        facts[slots + s] = place


def slot_ends(facts, slots):
    return [facts[s] for s in range(slots)]


def slot_mask(ends, slot, shape):
    rows = lax.broadcasted_iota(jnp.int32, shape, 1)
    inside = rows < ends[slot]
    if slot:
        inside = inside & (rows >= ends[slot - 1])
    return inside


def pick_slot(ends, products, rank):
    rows = lax.broadcasted_iota(jnp.int32, (rank, products.shape[1]), 1)
    slots = products.shape[0] // rank
    out = products[(slots - 1) * rank :]
    for s in range(slots - 2, -1, -1):
        out = jnp.where(rows < ends[s], products[s * rank : (s + 1) * rank], out)
    return out


def spread_slots(ends, values):
    wide = values.astype(f32)
    return jnp.concatenate(
        [jnp.where(slot_mask(ends, s, wide.shape), wide, 0.0) for s in range(len(ends))], axis=0
    ).astype(bf16)


def paired_sum(refs):
    parts = [ref[...] for ref in refs]
    while len(parts) > 1:
        parts = [parts[i] + parts[i + 1] for i in range(0, len(parts), 2)]
    return parts[0]


def select_kernel(slots, owned, tok_size, counts, placement, sequence, down, up, facts, *rest):
    ups, downs, sems = rest[:slots], rest[slots : 2 * slots], rest[2 * slots]
    facts_kernel(slots, owned, tok_size, counts, placement, sequence, facts)
    copies = []
    order = list(range(1, slots)) + [0]
    for s in order:
        copies.append(pltpu.make_async_copy(up.at[facts[slots + s]], ups[s], sems.at[s]))
    for s in order:
        copies.append(pltpu.make_async_copy(down.at[facts[slots + s]], downs[s], sems.at[slots + s]))
    for copy in copies:
        copy.start()
    for copy in copies:
        copy.wait()


def base_kernel(width, tokens, weight, keep, send):
    tp, sub = lax.axis_index("tp"), lax.axis_index("sub")
    mine, other = tp, 1 - tp
    for ref, s in ((send, 1 - sub), (keep, sub)):
        for i, t in enumerate((other, mine)):
            start = pl.multiple_of((t * 2 + s) * width, width)
            ref[i] = nn(tokens[...], weight[:, pl.ds(start, width)])


def stacked(tables):
    return jnp.concatenate([t[...] for t in tables], axis=0)


def back_kernel(slots, facts, grad, *rest):
    tables, out = rest[:slots], rest[slots]
    out[...] = pick_slot(slot_ends(facts, slots), nt(stacked(tables), grad[...]), ADAPTER_RANK)


def part_down_kernel(slots, pieces, facts, tokens, *rest):
    parts, spread_out, outs = rest[:pieces], rest[pieces], rest[pieces + 1 :]
    ends = slot_ends(facts, slots)
    back = (paired_sum(parts) * BACK_SCALE).astype(bf16)
    spread = spread_slots(ends, back)
    spread_out[...] = spread
    for c in range(0, tokens.shape[1], 256):
        columns = slice(c, min(c + 256, tokens.shape[1]))
        product = (nn(spread, tokens[:, columns]) * (adapter_scale * LOW_SCALE)).astype(bf16)
        for s in range(slots):
            outs[s][:, columns] = product[s * ADAPTER_RANK : (s + 1) * ADAPTER_RANK]


def low_kernel(slots, facts, tokens, *rest):
    tables, out = rest[:slots], rest[slots]
    out[...] = pick_slot(slot_ends(facts, slots), nt(stacked(tables), tokens[...]), ADAPTER_RANK)


def input_kernel(slots, width, spread, weight, *rest):
    tables, grads, (out, whole, turned) = rest[:slots], rest[slots:-3], rest[-3:]

    @pl.when(pl.program_id(0) == 0)
    def _():
        turned[...] = spread[...].astype(f32).T.astype(bf16)
        if len(grads) == 1:
            whole[...] = grads[0][...]
        else:
            tp, sub = lax.axis_index("tp"), lax.axis_index("sub")
            pieces = (grads[0][...], grads[1][...], grads[2][0], grads[2][1])
            for piece, t, s in zip(pieces, (tp, 1 - tp, tp, 1 - tp), (sub, sub, 1 - sub, 1 - sub)):
                start = pl.multiple_of((t * 2 + s) * width, width)
                whole[:, pl.ds(start, width)] = piece

    for c in range(0, out.shape[1], 256):
        columns = slice(c, min(c + 256, out.shape[1]))
        frozen = None
        for start in range(0, whole.shape[1], 256):
            term = nt(whole[:, start : start + 256], weight[columns, start : start + 256])
            frozen = term if frozen is None else frozen + term
        table = jnp.concatenate([t[:, columns] for t in tables], axis=0)
        adapter = nn(turned[...], table)
        out[:, columns] = (frozen + (adapter_scale * LOW_SCALE) * adapter).astype(bf16)


def second_kernel(slots, tok_size, pieces, facts, grad, *rest):
    parts, (spread_low, out) = rest[:pieces], rest[pieces:]
    me = lax.axis_index("tok")
    low = (paired_sum(parts) * LOW_SCALE).astype(bf16)
    spread = spread_slots(slot_ends(facts, slots), low)
    spread_low[...] = spread
    product = (nn(spread, grad[...]) * (adapter_scale * BACK_SCALE)).astype(bf16)
    for s in range(slots):
        out[lax.rem(me + s, tok_size)] = product[s * ADAPTER_RANK : (s + 1) * ADAPTER_RANK]


def adam_step(weights, mean_old, var_old, avg_old, gradient):
    mean_new = beta_one * mean_old + (1.0 - beta_one) * gradient
    var_new = beta_two * var_old + (1.0 - beta_two) * gradient * gradient
    root = var_new * lax.rsqrt(var_new) + adam_eps
    inverse = pl.reciprocal(root, approx=True)
    inverse = inverse * (2.0 - root * inverse)
    updated = weights.astype(f32) - learn_rate * mean_new * inverse
    return updated.astype(bf16), ema_decay * avg_old + (1.0 - ema_decay) * updated


def each_rows(count, body):
    rows = 16

    def step(i, _):
        body(pl.ds(pl.multiple_of(i * rows, rows), rows), rows)
        return 0

    lax.fori_loop(0, count // rows, step, 0)


def adam_kernel(slots, facts, *rest):
    came, old, rest = rest[:slots], rest[slots : slots + 4], rest[slots + 4 :]
    fresh, average, came_here = rest[:3]
    old_here, rest = rest[3:7], rest[7:]
    fresh_here, average_here, gradient_ref, in_sems, out_sems = rest
    owned, rank, width = fresh_here.shape

    arrivals = [
        pltpu.make_async_copy(came[s], came_here.at[s], in_sems.at[s]) for s in range(slots)
    ]
    loads, stores = [], []
    for k in range(owned):
        for i in range(4):
            sem = in_sems.at[slots + 4 * k + i]
            loads.append(pltpu.make_async_copy(old[i].at[k], old_here[i].at[k], sem))
        for i, (here, there) in enumerate(((fresh_here, fresh), (average_here, average))):
            sem = out_sems.at[2 * k + i]
            stores.append(pltpu.make_async_copy(here.at[k], there.at[k], sem))
    for copy in arrivals + loads:
        copy.start()

    for copy in arrivals:
        copy.wait()
    for k in range(owned):

        def clear(r, rows):
            gradient_ref[r, :] = jnp.zeros((rows, width), f32)

        each_rows(rank, clear)
        for s in range(slots):

            @pl.when(facts[slots + s] == k)
            def _():
                def add(r, rows):
                    gradient_ref[r, :] += came_here[s, r, :].astype(f32)

                each_rows(rank, add)

        for copy in loads[4 * k : 4 * k + 4]:
            copy.wait()

        def update(r, rows):
            for c in range(0, width, 512):
                columns = slice(c, min(c + 512, width))
                fresh_here[k, r, columns], average_here[k, r, columns] = adam_step(
                    *[ref[k, r, columns] for ref in old_here], gradient_ref[r, columns]
                )

        each_rows(rank, update)
        for copy in stores[2 * k : 2 * k + 2]:
            copy.start()
    for copy in stores:
        copy.wait()


def adam_down(facts, came, old):
    owned, rank, width = old[0].shape
    slots = len(came)
    shapes = [shape_of(old[0].shape, bf16), shape_of(old[0].shape, f32)]
    return pl.pallas_call(
        functools.partial(adam_kernel, slots),
        out_shape=shapes,
        in_specs=[SMEM] + [ANY] * (slots + 4),
        out_specs=[ANY] * 2,
        scratch_shapes=[pltpu.VMEM((slots, rank, width), bf16)]
        + [pltpu.VMEM(a.shape, a.dtype) for a in old]
        + [
            pltpu.VMEM(old[0].shape, bf16),
            pltpu.VMEM(old[0].shape, f32),
            pltpu.VMEM((rank, width), f32),
            pltpu.SemaphoreType.DMA((slots + 4 * owned,)),
            pltpu.SemaphoreType.DMA((2 * owned,)),
        ],
        compiler_params=params(60),
        cost_estimate=cost(owned * rank * width * 20, owned * rank * width * 60),
    )(facts, *came, *old)


def stack_kernel(own, across, out):
    out[0] = own[...]
    out[1] = across[...]


def stack_pair(own, across, flops):
    return pl.pallas_call(
        stack_kernel,
        out_shape=shape_of((2,) + own.shape, own.dtype),
        in_specs=[VMEM] * 2,
        out_specs=VMEM,
        compiler_params=params(16),
        cost_estimate=cost(flops, 2 * flops // 256),
    )(own, across)


def last_kernel(slots, tok_size, facts, came, *rest):
    old, rest = rest[:4], rest[4:]
    spread, tables, frozen = rest[0], rest[1 : 1 + slots], rest[1 + slots : -4]
    fresh, average, key_out, gradients = rest[-4:]
    raised = nn(spread[...].astype(f32).T.astype(bf16), stacked(tables))
    whole = frozen[0][...]
    for part in frozen[1:]:
        whole = whole + part[...].astype(f32)
    key_out[...] = (whole + (adapter_scale * BACK_SCALE) * raised).astype(bf16)
    me = lax.axis_index("tok")
    gradients[...] = jnp.zeros(gradients.shape, f32)
    for s in range(slots):
        gradients[facts[slots + s]] += came[lax.rem(me - s + tok_size, tok_size)].astype(f32)
    owned, rank, _ = gradients.shape
    for k in range(owned):

        def update(r, rows):
            fresh[k, r, :], average[k, r, :] = adam_step(
                *[ref[k, r, :] for ref in old], gradients[k, r, :]
            )

        each_rows(rank, update)


def last_step(facts, came, old, spread, tables, frozen, tok_size):
    shape = old[0].shape
    slots = len(tables)
    return pl.pallas_call(
        functools.partial(last_kernel, slots, tok_size),
        out_shape=[
            shape_of(shape, bf16),
            shape_of(shape, f32),
            shape_of(frozen[0].shape, bf16),
        ],
        in_specs=[SMEM] + [VMEM] * (6 + slots + len(frozen)),
        out_specs=[VMEM] * 3,
        scratch_shapes=[pltpu.VMEM(shape, f32)],
        compiler_params=params(16),
        cost_estimate=cost(old[0].size * 20, old[0].size * 20),
    )(facts, came, *old, spread, *tables, *frozen)


def after(value, *others):
    return lax.optimization_barrier((value, *others))[0]


def swap(block, axes, flips):
    sizes = [lax.axis_size(a) for a in axes]
    route = []
    for t in range(sizes[0]):
        for s in range(sizes[1]):
            source = (t ^ flips[0]) * sizes[1] + (s ^ flips[1])
            route.append((source, t * sizes[1] + s))
    return lax.ppermute(block, axes, route)


def per_device(
    tokens,
    frozen_key_weight,
    output_gradient,
    counts,
    placement,
    adapter_sequence,
    adapter_down,
    adapter_up,
    down_first_moment,
    down_second_moment,
    down_average,
    up_first_moment,
    up_second_moment,
    up_average,
):
    tok_size = lax.axis_size("tok")
    tp_size, sub_size = lax.axis_size("tp"), lax.axis_size("sub")
    shards = ("tp", "sub")
    square = tp_size == 2 and sub_size == 2
    rows, wide = tokens.shape
    narrow = output_gradient.shape[1]
    key_width = frozen_key_weight.shape[1]
    owned = adapter_down.shape[0]
    slots = placement.shape[1]
    rank = ADAPTER_RANK
    flip = lambda a: jnp.swapaxes(a, 1, 2)
    down, down_m, down_v, down_a = map(
        flip, (adapter_down, down_first_moment, down_second_moment, down_average)
    )
    up, up_m, up_v, up_a = map(flip, (adapter_up, up_first_moment, up_second_moment, up_average))

    def fetch(block, slot):
        return lax.ppermute(block, "tok", [((i + slot) % tok_size, i) for i in range(tok_size)])

    def give_back(block, slot):
        return lax.ppermute(block, "tok", [((i - slot) % tok_size, i) for i in range(tok_size)])

    def shared(part):
        if not square:
            return [lax.psum(part, shards)]
        both = part + swap(part, shards, (0, 1))
        return [both, swap(both, shards, (1, 0))]

    step = min(256, wide)

    facts, *sent = pl.pallas_call(
        functools.partial(select_kernel, slots, owned, tok_size),
        out_shape=[shape_of((2 * slots,), jnp.int32)]
        + [shape_of((rank, narrow), bf16)] * slots
        + [shape_of((rank, wide), bf16)] * slots,
        in_specs=[SMEM, SMEM, SMEM, ANY, ANY],
        out_specs=[SMEM] + [VMEM] * (2 * slots),
        scratch_shapes=[pltpu.SemaphoreType.DMA((2 * slots,))],
        compiler_params=params(56),
        cost_estimate=cost(0, 4 * slots * rank * (wide + narrow)),
    )(counts, placement, adapter_sequence, down, up)
    up_send, down_send = sent[:slots], sent[slots:]
    ready = counts[0, 0] > 0
    early = fetch(down_send[1], 1)
    up_tables = [up_send[0]] + [fetch(up_send[s], s) for s in range(1, slots)]
    if square:
        across = swap(after(output_gradient, facts), shards, (1, 0))
        pair = stack_pair(output_gradient, across, 2 * rows * wide * key_width)
        up_tables[0] = after(up_tables[0], pair)
    down_tables = [down_send[0], early] + [
        fetch(after(down_send[s], ready, early), s) for s in range(2, slots)
    ]
    up_tables[0] = after(up_tables[0], early)

    def group(work):
        shapes = jax.eval_shape(work)
        nothing = lambda: jax.tree.map(lambda a: jnp.zeros(a.shape, a.dtype), shapes)
        return lax.cond(ready, work, nothing)

    def back_work():
        part = pl.pallas_call(
            functools.partial(back_kernel, slots),
            out_shape=shape_of((rank, rows), f32),
            in_specs=[SMEM, VMEM] + [VMEM] * slots,
            out_specs=VMEM,
            compiler_params=params(16),
            cost_estimate=cost(2 * rows * narrow * rank * slots, 2 * rows * narrow),
        )(facts, output_gradient, *up_tables)
        parts = shared(part)
        if square:
            base = pl.pallas_call(
                functools.partial(base_kernel, narrow),
                out_shape=[shape_of((2, rows, narrow), f32)] * 2,
                in_specs=[VMEM, VMEM],
                out_specs=[VMEM, VMEM],
                compiler_params=params(16),
                cost_estimate=cost(2 * rows * wide * key_width, 2 * wide * (rows + key_width)),
            )(tokens, after(frozen_key_weight, parts[0]))
            grads = [swap(pair, shards, (0, 1))]
            parts = [after(parts[0], base[0]), parts[1]]
        else:
            base = []
            grads = [lax.all_gather(output_gradient, shards, axis=1, tiled=True)]
        spread, *sends = pl.pallas_call(
            functools.partial(part_down_kernel, slots, len(parts)),
            out_shape=[shape_of((slots * rank, rows), bf16)] + [shape_of((rank, wide), bf16)] * slots,
            in_specs=[SMEM, VMEM] + [VMEM] * len(parts),
            out_specs=[VMEM] * (1 + slots),
            compiler_params=params(16),
            cost_estimate=cost(2 * rows * wide * rank * slots, 2 * rows * wide),
        )(facts, tokens, *parts)
        return grads, base, spread, sends

    grads, base, spread_back, part_down = group(back_work)
    if square:
        grads = [output_gradient, across] + grads
    came = {0: part_down[0]}
    for s in sorted(range(1, slots), key=lambda s: s == 2):
        early = [] if s == 2 else down_tables[1:]
        came[s] = give_back(after(part_down[s], *early), s)
    came = [came[s] for s in range(slots)]

    wide_step = min(512, wide)

    def input_whole(spread):
        return pl.pallas_call(
            functools.partial(input_kernel, slots, narrow),
            grid=(wide // wide_step,),
            out_shape=shape_of((rows, wide), bf16),
            in_specs=[
                pl.BlockSpec((slots * rank, rows), lambda i: (0, 0)),
                pl.BlockSpec((wide_step, key_width), lambda i: (i, 0)),
            ]
            + [pl.BlockSpec((rank, wide_step), lambda i: (0, i))] * slots
            + [pl.BlockSpec(g.shape, lambda i, r=g.ndim: (0,) * r) for g in grads],
            out_specs=pl.BlockSpec((rows, wide_step), lambda i: (0, i)),
            scratch_shapes=[
                pltpu.VMEM((rows, key_width), bf16),
                pltpu.VMEM((rows, slots * rank), bf16),
            ],
            compiler_params=params(16),
            cost_estimate=cost(
                2 * rows * wide * (key_width + rank * slots), 2 * wide * (rows + key_width)
            ),
        )(spread, frozen_key_weight, *down_tables, *grads)

    def low_work():
        part = pl.pallas_call(
            functools.partial(low_kernel, slots),
            out_shape=shape_of((rank, rows), f32),
            in_specs=[SMEM, VMEM] + [VMEM] * slots,
            out_specs=VMEM,
            compiler_params=params(16),
            cost_estimate=cost(2 * rows * wide * rank * slots, 2 * rows * wide),
        )(facts, tokens, *down_tables)
        parts = shared(part)
        input_gradient = input_whole(after(spread_back, parts[0]))
        if square:
            keep, send = base
            got = swap(send, shards, (0, 1))
            frozen, passing = keep[1] + got[1], (keep[0] + got[0]).astype(bf16)
            parts = [after(parts[0], input_gradient, frozen, passing), parts[1]]
        else:
            whole = jnp.dot(tokens, frozen_key_weight, preferred_element_type=f32)
            frozen = lax.psum_scatter(whole, shards, scatter_dimension=1, tiled=True)
            passing = ()
        spread, send = pl.pallas_call(
            functools.partial(second_kernel, slots, tok_size, len(parts)),
            out_shape=[
                shape_of((slots * rank, rows), bf16),
                shape_of((tok_size, rank, narrow), bf16),
            ],
            in_specs=[SMEM] + [VMEM] * (1 + len(parts)),
            out_specs=[VMEM] * 2,
            compiler_params=params(16),
            cost_estimate=cost(2 * rows * narrow * rank * slots, 2 * rows * narrow),
        )(facts, output_gradient, *parts)
        return spread, send, frozen, passing, input_gradient

    spread_low, part_up, frozen, passing, input_gradient = group(low_work)
    came_up = lax.all_to_all(part_up, "tok", split_axis=0, concat_axis=0, tiled=True)
    frozen = [frozen]
    if square:
        frozen.append(swap(passing, shards, (1, 0)))

    fresh_down, average_down = adam_down(facts, came, (down, down_m, down_v, down_a))
    fresh_up, average_up, key_output = last_step(
        facts,
        after(came_up, fresh_down),
        (up, up_m, up_v, up_a),
        spread_low,
        up_tables,
        frozen,
        tok_size,
    )
    return (
        key_output,
        input_gradient,
        flip(fresh_down),
        flip(fresh_up),
        flip(average_down),
        flip(average_up),
    )


def solution(mesh):
    rows = P(("groups", "tok"), ("tp", "sub"))
    cube = P(("groups", "tok"), ("tp", "sub"), None)
    return jax.shard_map(
        per_device,
        mesh=mesh,
        in_specs=(rows, P(("tp", "sub"), None), rows, P("groups", None), P("groups", None), P("groups"))
        + (cube,) * 8,
        out_specs=(rows, rows, cube, cube, cube, cube),
        check_vma=False,
    )
```

profile of v0, /device:TPU:0, one launch (start us, length us, event | category | flops | bytes accessed | tf_op | source)
XLA Modules:
  0.0 64.7 jit_solution(3942207363359753834)
XLA Ops:
  0.6 3.1 %shard_map.181 = (s32[8]{0:T(128)S(1)}, bf16[64,256]{1,0:T(8,128)(2,1)S(1)}, bf16[64,256]{1,0:T(8,128)(2,1)}, bf16[64,256]{1,0:T(8,128)(2,1)}, bf16[64,256]{1,0:...) custom-call(s32[4,4]{1,0:T(4,128)} %counts.1, ...), custom_call_target="tpu_custom_call" | custom-call | bytes 7077888 | tf_op jit(solution)/shard_map/pallas_call | solution.py:416
  3.7 5.1 %collective-permute-start.6 = (bf16[64,2048]{1,0:T(8,128)(2,1)}, bf16[64,2048]{1,0:T(8,128)(2,1)S(1)}, u32[]{:S(2)}, u32[]{:S(2)}) collective-permute-start(bf16[64,2048]{1,0:T(8,128)(2,1)} %get-tuple-element.122), channel_id=1, source_target_pairs={{4,0},{8,4},{12,8},{0,12},{5,1},{9,5},{13,9},{1,13},{6,2},{10,6},{... | collective-permute-start | bytes 786440 | tf_op jit(solution)/shard_map/ppermute | solution.py:403
  8.8 1.5 %collective-permute-start.9 = (bf16[512,256]{1,0:T(8,128)(2,1)}, bf16[512,256]{1,0:T(8,128)(2,1)S(1)}, u32[]{:S(2)}, u32[]{:S(2)}) collective-permute-start(bf16[512,256]{1,0:T(8,128)(2,1)} %own.1), channel_id=1, source_target_pairs={{2,0},{3,1},{0,2},{1,3},{6,4},{7,5},{4,6},{5,7},{10,8},{11,9},{8,1... | collective-permute-start | bytes 786440 | tf_op jit(solution)/shard_map/ppermute | solution.py:367
  10.3 0.4 collective-permute-start.10
  10.8 0.0 collective-permute-start.11
  10.8 1.6 %collective-permute-start.12 = (bf16[64,256]{1,0:T(8,128)(2,1)}, bf16[64,256]{1,0:T(8,128)(2,1)S(1)}, u32[]{:S(2)}, u32[]{:S(2)}) collective-permute-start(bf16[64,256]{1,0:T(8,128)(2,1)} %get-tuple-element.133), channel_id=1, source_target_pairs={{12,0},{0,4},{4,8},{8,12},{13,1},{1,5},{5,9},{9,13},{14,2},{2,6},{... | collective-permute-start | bytes 98312 | tf_op jit(solution)/shard_map/ppermute | solution.py:403
  12.4 1.2 %slice.15 = s32[1,1]{1,0:T(1,128)} slice(s32[4,4]{1,0:T(4,128)} %counts.1), slice={[0:1], [0:1]} | slice | bytes 8 | tf_op jit(solution)/shard_map/slice | solution.py:428
  14.2 1.7 %collective-permute-done.6 = bf16[64,2048]{1,0:T(8,128)(2,1)S(1)} collective-permute-done((bf16[64,2048]{1,0:T(8,128)(2,1)}, bf16[64,2048]{1,0:T(8,128)(2,1)S(1)}, u32[]{:S(2)}, u32[]{:S(2)}) %collective-permute-start.6) | collective-permute-done | bytes 262176 | tf_op jit(solution)/shard_map/ppermute | solution.py:403
  15.9 1.4 %collective-permute-start.7 = (bf16[64,2048]{1,0:T(8,128)(2,1)}, bf16[64,2048]{1,0:T(8,128)(2,1)}, u32[]{:S(2)}, u32[]{:S(2)}) collective-permute-start(bf16[64,2048]{1,0:T(8,128)(2,1)} %get-tuple-element.124), channel_id=1, source_target_pairs={{8,0},{12,4},{0,8},{4,12},{9,1},{13,5},{1,9},{5,13},{10,2},{14,6},... | collective-permute-start | bytes 786440 | tf_op jit(solution)/shard_map/ppermute | solution.py:403
  17.3 3.5 %collective-permute-start.8 = (bf16[64,2048]{1,0:T(8,128)(2,1)}, bf16[64,2048]{1,0:T(8,128)(2,1)}, u32[]{:S(2)}, u32[]{:S(2)}) collective-permute-start(bf16[64,2048]{1,0:T(8,128)(2,1)} %get-tuple-element.126), channel_id=1, source_target_pairs={{12,0},{0,4},{4,8},{8,12},{13,1},{1,5},{5,9},{9,13},{14,2},{2,6},{... | collective-permute-start | bytes 786440 | tf_op jit(solution)/shard_map/ppermute | solution.py:403
  20.7 1.0 %shard_map.182 = bf16[2,512,256]{2,1,0:T(8,128)(2,1)S(1)} custom-call(bf16[512,256]{1,0:T(8,128)(2,1)} %own.1, bf16[512,256]{1,0:T(8,128)(2,1)S(1)} %collective-permute-done.9.across), custom_call_target="tpu_custom_call" | custom-call | flops 6442450944 | bytes 50331648 | tf_op jit(solution)/shard_map/pallas_call | solution.py:304
  21.7 0.0 collective-permute-done.10.rest_6_
  21.8 10.0 %conditional.2 = (bf16[2,512,256]{2,1,0:T(8,128)(2,1)}, f32[2,512,256]{2,1,0:T(8,128)S(1)}, f32[2,512,256]{2,1,0:T(8,128)S(1)}, bf16[256,512]{1,0:T(8,128)(2,1)S...) conditional(s32[]{:T(128)} %convert_element_type.10, () %tuple.39, ...), branch_computations={%region_0.0_spmd, %region_1.0_spmd} | conditional | flops 8254423040 | bytes 29491384 | solution.py:443
  21.8 0.8 %branch_1_fun.6 = f32[64,512]{1,0:T(8,128)S(1)} custom-call(s32[8]{0:T(128)S(1)} %get-tuple-element.47.facts, bf16[512,256]{1,0:T(8,128)(2,1)S(1)} %get-tuple-element.48.grad, bf16[64,256]{1,0:T(8,128)(2,1)S(1)} %get-tuple-element.49.rest_0_, bf16[64,256]{1,0:T(8,128)(2,1)S(1)} %get-tuple-element.50.rest_1_, bf16[64,256]{1,0:T(8,128)(2,1)S(1)} %get-tuple-element.51.rest_2_, ...), custom_call_target="tpu_custom_call" | custom-call | flops 201326592 | bytes 786432 | tf_op jit(solution)/shard_map/cond/branch_1_fun/pallas_call | solution.py:446
  22.6 0.1 collective-permute-start.1
  22.7 0.5 collective-permute-start
  23.2 0.8 %collective-permute-done.1 = f32[64,512]{1,0:T(8,128)S(1)} collective-permute-done((f32[64,512]{1,0:T(8,128)S(1)}, f32[64,512]{1,0:T(8,128)S(1)}, u32[]{:S(2)}, u32[]{:S(2)}) %collective-permute-start.1) | collective-permute-done | bytes 131104 | tf_op jit(solution)/shard_map/cond/branch_1_fun/ppermute | solution.py:367
  24.1 1.6 %collective-permute-start.2 = (f32[64,512]{1,0:T(8,128)S(1)}, f32[64,512]{1,0:T(8,128)S(1)}, u32[]{:S(2)}, u32[]{:S(2)}) collective-permute-start(f32[64,512]{1,0:T(8,128)S(1)} %add.11.rest_0_), channel_id=1, source_target_pairs={{2,0},{3,1},{0,2},{1,3},{6,4},{7,5},{4,6},{5,7},{10,8},{11,9},{8,1... | collective-permute-start | bytes 393224 | tf_op jit(solution)/shard_map/cond/branch_1_fun/ppermute | solution.py:367
  25.7 2.4 %branch_1_fun.7 = (f32[2,512,256]{2,1,0:T(8,128)S(1)}, f32[2,512,256]{2,1,0:T(8,128)S(1)}) custom-call(bf16[512,2048]{1,0:T(8,128)(2,1)S(1)} %get-tuple-element.45.tokens, bf16[2048,1024]{1,0:T(8,128)(2,1)S(1)} %get-tuple-element.53.weight), custom_call_target="tpu_custom_call" | custom-call | flops 6442450944 | bytes 18874368 | tf_op jit(solution)/shard_map/cond/branch_1_fun/pallas_call | solution.py:456
  28.0 1.6 %collective-permute-done.2.rest_1_ = f32[64,512]{1,0:T(8,128)S(1)} collective-permute-done((f32[64,512]{1,0:T(8,128)S(1)}, f32[64,512]{1,0:T(8,128)S(1)}, u32[]{:S(2)}, u32[]{:S(2)}) %collective-permute-start.2) | collective-permute-done | bytes 131104 | tf_op jit(solution)/shard_map/cond/branch_1_fun/ppermute | solution.py:367
  29.7 2.1 %branch_1_fun.8 = (bf16[256,512]{1,0:T(8,128)(2,1)S(1)}, bf16[64,2048]{1,0:T(8,128)(2,1)S(1)}, bf16[64,2048]{1,0:T(8,128)(2,1)}, bf16[64,2048]{1,0:T(8,128)(2,1)}, bf16[64,2048]{1,0:T(8,128)(2,1)}) custom-call(s32[8]{0:T(128)S(1)} %get-tuple-element.47.facts, bf16[512,2048]{1,0:T(8,128)(2,1)S(1)} %get-tuple-element.45.tokens, f32[64,512]{1,0:T(8,128)S(1)} %add.11.rest_0_, ...), custom_call_target="tpu_custom_call" | custom-call | flops 1610612736 | bytes 6291456 | tf_op jit(solution)/shard_map/cond/branch_1_fun/pallas_call | solution.py:469
  31.8 0.0 collective-permute-done
  31.8 3.7 %collective-permute-start.14 = (bf16[64,2048]{1,0:T(8,128)(2,1)}, bf16[64,2048]{1,0:T(8,128)(2,1)}, u32[]{:S(2)}, u32[]{:S(2)}) collective-permute-start(bf16[64,2048]{1,0:T(8,128)(2,1)} %get-tuple-element.142), channel_id=1, source_target_pairs={{8,0},{12,4},{0,8},{4,12},{9,1},{13,5},{1,9},{5,13},{10,2},{14,6},... | collective-permute-start | bytes 786440 | tf_op jit(solution)/shard_map/ppermute | solution.py:406
  35.5 0.2 collective-permute-start.15
  35.7 1.8 %collective-permute-start.13 = (bf16[64,2048]{1,0:T(8,128)(2,1)}, bf16[64,2048]{1,0:T(8,128)(2,1)}, u32[]{:S(2)}, u32[]{:S(2)}) collective-permute-start(bf16[64,2048]{1,0:T(8,128)(2,1)} %get-tuple-element.141), channel_id=1, source_target_pairs={{12,0},{0,4},{4,8},{8,12},{13,1},{1,5},{5,9},{9,13},{14,2},{2,6},{... | collective-permute-start | bytes 786440 | tf_op jit(solution)/shard_map/ppermute | solution.py:406
  37.6 13.5 %conditional.3 = (bf16[256,512]{1,0:T(8,128)(2,1)S(1)}, bf16[4,64,256]{2,1,0:T(8,128)(2,1)}, f32[512,256]{1,0:T(8,128)S(1)}, bf16[512,256]{1,0:T(8,128)(2,1)}, bf16[512,2048]{1,0:T(8,128)(2,1)S(1)}) conditional(s32[]{:T(128)} %convert_element_type.10, () %tuple.36, (s32[8]{0:T(128)S(1)}, bf16[512,2048]{1,0:T(8,128)(2,1)}, bf16[64,2048]{1,0:T(8,128)(2,1)}, ...), branch_computations={%region_2.0_spmd, %region_3.0_spmd} | conditional | flops 9865428992 | bytes 56492360 | solution.py:443
  37.6 0.0 collective-permute-start.4
  37.6 0.0 copy-start.13
  37.6 0.0 copy-start.15
  37.6 2.7 %branch_1_fun.9 = f32[64,512]{1,0:T(8,128)S(1)} custom-call(s32[8]{0:T(128)S(1)} %get-tuple-element.62.facts, bf16[512,2048]{1,0:T(8,128)(2,1)} %get-tuple-element.64.tokens, bf16[64,2048]{1,0:T(8,128)(2,1)} %get-tuple-element.65.rest_0_, bf16[64,2048]{1,0:T(8,128)(2,1)} %get-tuple-element.66.rest_1_, bf16[64,2048]{1,0:T(8,128)(2,1)} %get-tuple-element.67.rest_2_, ...), custom_call_target="tpu_custom_call" | custom-call | flops 1610612736 | bytes 6291456 | tf_op jit(solution)/shard_map/cond/branch_1_fun/pallas_call | solution.py:513
  40.3 0.6 collective-permute-start.3
  40.9 1.0 %collective-permute-done.3 = f32[64,512]{1,0:T(8,128)S(1)} collective-permute-done((f32[64,512]{1,0:T(8,128)S(1)}, f32[64,512]{1,0:T(8,128)S(1)}, u32[]{:S(2)}, u32[]{:S(2)}) %collective-permute-start.3) | collective-permute-done | bytes 131104 | tf_op jit(solution)/shard_map/cond/branch_1_fun/ppermute | solution.py:367
  41.9 1.6 %collective-permute-start.5 = (f32[64,512]{1,0:T(8,128)S(1)}, f32[64,512]{1,0:T(8,128)S(1)}, u32[]{:S(2)}, u32[]{:S(2)}) collective-permute-start(f32[64,512]{1,0:T(8,128)S(1)} %add.12.rest_0_), channel_id=1, source_target_pairs={{2,0},{3,1},{0,2},{1,3},{6,4},{7,5},{4,6},{5,7},{10,8},{11,9},{8,1... | collective-permute-start | bytes 393224 | tf_op jit(solution)/shard_map/cond/branch_1_fun/ppermute | solution.py:367
  43.5 5.1 %branch_1_fun.10 = bf16[512,2048]{1,0:T(8,128)(2,1)S(1)} custom-call(bf16[256,512]{1,0:T(8,128)(2,1)S(1)} %get-tuple-element.70.spread, bf16[2048,1024]{1,0:T(8,128)(2,1)S(1)} %copy-done.6, bf16[64,2048]{1,0:T(8,128)(2,1)S(1)} %copy-done.11, bf16[64,2048]{1,0:T(8,128)(2,1)S(1)} %copy-done.13, bf16[64,2048]{1,0:T(8,128)(2,1)} %get-tuple-element.67.rest_2_, ...), custom_call_target="tpu_custom_call" | custom-call | flops 8053063680 | bytes 18874368 | tf_op jit(solution)/shard_map/cond/branch_1_fun/pallas_call | solution.py:491
  48.6 0.0 copy-start.10
  48.6 0.8 %fusion.2 = (bf16[512,256]{1,0:T(8,128)(2,1)}, f32[512,256]{1,0:T(8,128)S(1)}) fusion(f32[2,512,256]{2,1,0:T(8,128)S(1)} %collective-permute-done.4, f32[2,512,256]{2,1,0:T(8,128)S(1)} %get-tuple-element.74), kind=kLoop, calls=%fused_computation.4 | loop fusion | flops 393216 | bytes 2883584 | tf_op jit(solution)/shard_map/cond/branch_1_fun/convert_element_type | solution.py:526
  49.5 0.1 copy-done.10
  49.6 1.4 %branch_1_fun.11 = (bf16[256,512]{1,0:T(8,128)(2,1)S(1)}, bf16[4,64,256]{2,1,0:T(8,128)(2,1)}) custom-call(s32[8]{0:T(128)S(1)} %get-tuple-element.62.facts, bf16[512,256]{1,0:T(8,128)(2,1)S(1)} %copy-done.10, f32[64,512]{1,0:T(8,128)S(1)} %add.12.rest_0_, f32[64,512]{1,0:T(8,128)S(1)} %collective-permute-done.5.rest_1_), custom_call_target="tpu_custom_call" | custom-call | flops 201326592 | bytes 786432 | tf_op jit(solution)/shard_map/cond/branch_1_fun/pallas_call | solution.py:532
  51.0 1.3 %copy-done.4 = bf16[512,2048]{1,0:T(8,128)(2,1)} copy-done((bf16[512,2048]{1,0:T(8,128)(2,1)}, bf16[512,2048]{1,0:T(8,128)(2,1)S(1)}, u32[]{:S(2)}) %copy-start.4) | copy-done | bytes 2097176
  52.3 0.5 collective-permute-start.16
  52.8 3.6 %all-to-all-start = ((bf16[4,64,256]{2,1,0:T(8,128)(2,1)}), bf16[4,64,256]{2,1,0:T(8,128)(2,1)S(1)}, u32[]{:S(2)}, u32[]{:S(2)}) async-start(bf16[4,64,256]{2,1,0:T(8,128)(2,1)} %get-tuple-element.138), calls=%async_computation | async-start | bytes 262144 | tf_op jit(solution)/shard_map/all_to_all | solution.py:546
  56.5 0.0 copy-start
  56.5 0.0 copy-start.1
  56.5 0.0 copy-start.2
  56.5 0.0 copy-start.3
  56.5 5.7 %shard_map.183 = (bf16[4,64,2048]{2,1,0:T(8,128)(2,1)}, f32[4,64,2048]{2,1,0:T(8,128)}) custom-call(s32[8]{0:T(128)S(1)} %get-tuple-element.120.facts, bf16[64,2048]{1,0:T(8,128)(2,1)S(1)} %get-tuple-element.139.rest_0_, bf16[64,2048]{1,0:T(8,128)(2,1)} %collective-permute-done.13.rest_1_, bf16[64,2048]{1,0:T(8,128)(2,1)} %collective-permute-done.14.rest_2_, ...), custom_call_target="tpu_custom_call" | custom-call | flops 31457280 | bytes 94371840 | tf_op jit(solution)/shard_map/pallas_call | solution.py:279
  62.3 0.3 all-to-all-done.came
  62.6 2.1 %shard_map.184 = (bf16[4,64,256]{2,1,0:T(8,128)(2,1)}, f32[4,64,256]{2,1,0:T(8,128)}, bf16[512,256]{1,0:T(8,128)(2,1)}) custom-call(s32[8]{0:T(128)S(1)} %get-tuple-element.120.facts, bf16[4,64,256]{2,1,0:T(8,128)(2,1)S(1)} %all-to-all-done.came, bf16[4,64,256]{2,1,0:T(8,128)(2,1)S(1)} %bitcast.18, f32[4,64,256]{2,1,0:T(8,128)S(1)} %bitcast.19, ...), custom_call_target="tpu_custom_call" | custom-call | flops 3932160 | bytes 3932160 | tf_op jit(solution)/shard_map/pallas_call | solution.py:341
  (36 shorter events, 0.1 us)
Async XLA Ops:
  3.7 12.1 %collective-permute-start.6 = (bf16[64,2048]{1,0:T(8,128)(2,1)}, bf16[64,2048]{1,0:T(8,128)(2,1)S(1)}, u32[]{:S(2)}, u32[]{:S(2)}) collective-permute-start(bf16[64,2048]{1,0:T(8,128)(2,1)} %get-tuple-element.122), channel_id=1, source_target_pairs={{4,0},{8,4},{12,8},{0,12},{5,1},{9,5},{13,9},{1,13},{6,2},{10,6},{... | collective-permute-start | bytes 786440 | tf_op jit(solution)/shard_map/ppermute | solution.py:403
  8.8 8.4 %collective-permute-start.9 = (bf16[512,256]{1,0:T(8,128)(2,1)}, bf16[512,256]{1,0:T(8,128)(2,1)S(1)}, u32[]{:S(2)}, u32[]{:S(2)}) collective-permute-start(bf16[512,256]{1,0:T(8,128)(2,1)} %own.1), channel_id=1, source_target_pairs={{2,0},{3,1},{0,2},{1,3},{6,4},{7,5},{4,6},{5,7},{10,8},{11,9},{8,1... | collective-permute-start | bytes 786440 | tf_op jit(solution)/shard_map/ppermute | solution.py:367
  10.3 11.4 %collective-permute-start.10 = (bf16[64,256]{1,0:T(8,128)(2,1)}, bf16[64,256]{1,0:T(8,128)(2,1)S(1)}, u32[]{:S(2)}, u32[]{:S(2)}) collective-permute-start(bf16[64,256]{1,0:T(8,128)(2,1)} %get-tuple-element.131), channel_id=1, source_target_pairs={{4,0},{8,4},{12,8},{0,12},{5,1},{9,5},{13,9},{1,13},{6,2},{10,6},{... | collective-permute-start | bytes 98312 | tf_op jit(solution)/shard_map/ppermute | solution.py:403
  10.8 11.0 %collective-permute-start.11 = (bf16[64,256]{1,0:T(8,128)(2,1)}, bf16[64,256]{1,0:T(8,128)(2,1)S(1)}, u32[]{:S(2)}, u32[]{:S(2)}) collective-permute-start(bf16[64,256]{1,0:T(8,128)(2,1)} %get-tuple-element.132), channel_id=1, source_target_pairs={{8,0},{12,4},{0,8},{4,12},{9,1},{13,5},{1,9},{5,13},{10,2},{14,6},... | collective-permute-start | bytes 98312 | tf_op jit(solution)/shard_map/ppermute | solution.py:403
  10.8 11.0 %collective-permute-start.12 = (bf16[64,256]{1,0:T(8,128)(2,1)}, bf16[64,256]{1,0:T(8,128)(2,1)S(1)}, u32[]{:S(2)}, u32[]{:S(2)}) collective-permute-start(bf16[64,256]{1,0:T(8,128)(2,1)} %get-tuple-element.133), channel_id=1, source_target_pairs={{12,0},{0,4},{4,8},{8,12},{13,1},{1,5},{5,9},{9,13},{14,2},{2,6},{... | collective-permute-start | bytes 98312 | tf_op jit(solution)/shard_map/ppermute | solution.py:403
  15.9 5.9 %copy-start.12 = (bf16[64,2048]{1,0:T(8,128)(2,1)}, bf16[64,2048]{1,0:T(8,128)(2,1)S(1)}, u32[]{:S(2)}) copy-start(bf16[64,2048]{1,0:T(8,128)(2,1)S(1)} %collective-permute-done.6) | copy-start | bytes 786436
  15.9 5.9 %copy-start.5 = (bf16[2048,1024]{1,0:T(8,128)(2,1)S(1)}, bf16[2048,1024]{1,0:T(8,128)(2,1)}, u32[]{:S(2)}) copy-start(bf16[2048,1024]{1,0:T(8,128)(2,1)} %param.19) | copy-start | bytes 12582916
  15.9 5.9 %copy-start.7 = (bf16[512,2048]{1,0:T(8,128)(2,1)S(1)}, bf16[512,2048]{1,0:T(8,128)(2,1)}, u32[]{:S(2)}) copy-start(bf16[512,2048]{1,0:T(8,128)(2,1)} %param.18) | copy-start | bytes 6291460
  15.9 5.9 %copy-start.8 = (bf16[512,256]{1,0:T(8,128)(2,1)S(1)}, bf16[512,256]{1,0:T(8,128)(2,1)}, u32[]{:S(2)}) copy-start(bf16[512,256]{1,0:T(8,128)(2,1)} %own.1) | copy-start | bytes 786436
  15.9 19.6 %collective-permute-start.7 = (bf16[64,2048]{1,0:T(8,128)(2,1)}, bf16[64,2048]{1,0:T(8,128)(2,1)}, u32[]{:S(2)}, u32[]{:S(2)}) collective-permute-start(bf16[64,2048]{1,0:T(8,128)(2,1)} %get-tuple-element.124), channel_id=1, source_target_pairs={{8,0},{12,4},{0,8},{4,12},{9,1},{13,5},{1,9},{5,13},{10,2},{14,6},... | collective-permute-start | bytes 786440 | tf_op jit(solution)/shard_map/ppermute | solution.py:403
  17.3 4.5 %copy-start.14 = (bf16[512,256]{1,0:T(8,128)(2,1)}, bf16[512,256]{1,0:T(8,128)(2,1)S(1)}, u32[]{:S(2)}) copy-start(bf16[512,256]{1,0:T(8,128)(2,1)S(1)} %collective-permute-done.9.across) | copy-start | bytes 786436
  17.3 18.3 %collective-permute-start.8 = (bf16[64,2048]{1,0:T(8,128)(2,1)}, bf16[64,2048]{1,0:T(8,128)(2,1)}, u32[]{:S(2)}, u32[]{:S(2)}) collective-permute-start(bf16[64,2048]{1,0:T(8,128)(2,1)} %get-tuple-element.126), channel_id=1, source_target_pairs={{12,0},{0,4},{4,8},{8,12},{13,1},{1,5},{5,9},{9,13},{14,2},{2,6},{... | collective-permute-start | bytes 786440 | tf_op jit(solution)/shard_map/ppermute | solution.py:403
  22.6 1.4 %collective-permute-start.1 = (f32[64,512]{1,0:T(8,128)S(1)}, f32[64,512]{1,0:T(8,128)S(1)}, u32[]{:S(2)}, u32[]{:S(2)}) collective-permute-start(f32[64,512]{1,0:T(8,128)S(1)} %branch_1_fun.6), channel_id=1, source_target_pairs={{1,0},{0,1},{3,2},{2,3},{5,4},{4,5},{7,6},{6,7},{9,8},{8,9},{11,10... | collective-permute-start | bytes 393224 | tf_op jit(solution)/shard_map/cond/branch_1_fun/ppermute | solution.py:367
  22.7 9.1 %collective-permute-start = (bf16[2,512,256]{2,1,0:T(8,128)(2,1)S(1)}, bf16[2,512,256]{2,1,0:T(8,128)(2,1)}, u32[]{:S(2)}, u32[]{:S(2)}) collective-permute-start(bf16[2,512,256]{2,1,0:T(8,128)(2,1)S(1)} %get-tuple-element.44), channel_id=1, source_target_pairs={{1,0},{0,1},{3,2},{2,3},{5,4},{4,5},{7,6},{6,7},{9,8},{8,9},{11,10... | collective-permute-start | bytes 1572872 | tf_op jit(solution)/shard_map/cond/branch_1_fun/ppermute | solution.py:367
  24.1 5.6 %collective-permute-start.2 = (f32[64,512]{1,0:T(8,128)S(1)}, f32[64,512]{1,0:T(8,128)S(1)}, u32[]{:S(2)}, u32[]{:S(2)}) collective-permute-start(f32[64,512]{1,0:T(8,128)S(1)} %add.11.rest_0_), channel_id=1, source_target_pairs={{2,0},{3,1},{0,2},{1,3},{6,4},{7,5},{4,6},{5,7},{10,8},{11,9},{8,1... | collective-permute-start | bytes 393224 | tf_op jit(solution)/shard_map/cond/branch_1_fun/ppermute | solution.py:367
  31.8 24.7 %collective-permute-start.14 = (bf16[64,2048]{1,0:T(8,128)(2,1)}, bf16[64,2048]{1,0:T(8,128)(2,1)}, u32[]{:S(2)}, u32[]{:S(2)}) collective-permute-start(bf16[64,2048]{1,0:T(8,128)(2,1)} %get-tuple-element.142), channel_id=1, source_target_pairs={{8,0},{12,4},{0,8},{4,12},{9,1},{13,5},{1,9},{5,13},{10,2},{14,6},... | collective-permute-start | bytes 786440 | tf_op jit(solution)/shard_map/ppermute | solution.py:406
  35.5 21.0 %collective-permute-start.15 = (bf16[64,2048]{1,0:T(8,128)(2,1)}, bf16[64,2048]{1,0:T(8,128)(2,1)}, u32[]{:S(2)}, u32[]{:S(2)}) collective-permute-start(bf16[64,2048]{1,0:T(8,128)(2,1)} %get-tuple-element.144), channel_id=1, source_target_pairs={{4,0},{8,4},{12,8},{0,12},{5,1},{9,5},{13,9},{1,13},{6,2},{10,6},{... | collective-permute-start | bytes 786440 | tf_op jit(solution)/shard_map/ppermute | solution.py:406
  35.7 20.8 %collective-permute-start.13 = (bf16[64,2048]{1,0:T(8,128)(2,1)}, bf16[64,2048]{1,0:T(8,128)(2,1)}, u32[]{:S(2)}, u32[]{:S(2)}) collective-permute-start(bf16[64,2048]{1,0:T(8,128)(2,1)} %get-tuple-element.141), channel_id=1, source_target_pairs={{12,0},{0,4},{4,8},{8,12},{13,1},{1,5},{5,9},{9,13},{14,2},{2,6},{... | collective-permute-start | bytes 786440 | tf_op jit(solution)/shard_map/ppermute | solution.py:406
  37.6 5.9 %copy-start.9 = (bf16[512,256]{1,0:T(8,128)(2,1)}, bf16[512,256]{1,0:T(8,128)(2,1)S(1)}, u32[]{:S(2)}) copy-start(bf16[512,256]{1,0:T(8,128)(2,1)S(1)} %get-tuple-element.63.rest_4_.grad) | copy-start | bytes 786436 | tf_op jit(solution)/shard_map/cond
  37.6 11.1 %collective-permute-start.4 = (f32[2,512,256]{2,1,0:T(8,128)S(1)}, f32[2,512,256]{2,1,0:T(8,128)S(1)}, u32[]{:S(2)}, u32[]{:S(2)}) collective-permute-start(f32[2,512,256]{2,1,0:T(8,128)S(1)} %get-tuple-element.75), channel_id=1, source_target_pairs={{1,0},{0,1},{3,2},{2,3},{5,4},{4,5},{7,6},{6,7},{9,8},{8,9},{11,10... | collective-permute-start | bytes 3145736 | tf_op jit(solution)/shard_map/cond/branch_1_fun/ppermute | solution.py:367
  37.6 5.9 %copy-start.6 = (bf16[2048,1024]{1,0:T(8,128)(2,1)S(1)}, bf16[2048,1024]{1,0:T(8,128)(2,1)}, u32[]{:S(2)}) copy-start(bf16[2048,1024]{1,0:T(8,128)(2,1)} %get-tuple-element.71.weight) | copy-start | bytes 12582916 | tf_op jit(solution)/shard_map/cond
  37.6 5.9 %copy-start.11 = (bf16[64,2048]{1,0:T(8,128)(2,1)S(1)}, bf16[64,2048]{1,0:T(8,128)(2,1)}, u32[]{:S(2)}) copy-start(bf16[64,2048]{1,0:T(8,128)(2,1)} %get-tuple-element.65.rest_0_) | copy-start | bytes 786436 | tf_op jit(solution)/shard_map/cond
  37.6 5.9 %copy-start.13 = (bf16[64,2048]{1,0:T(8,128)(2,1)S(1)}, bf16[64,2048]{1,0:T(8,128)(2,1)}, u32[]{:S(2)}) copy-start(bf16[64,2048]{1,0:T(8,128)(2,1)} %get-tuple-element.66.rest_1_) | copy-start | bytes 786436 | tf_op jit(solution)/shard_map/cond
  37.6 5.9 %copy-start.15 = (bf16[512,256]{1,0:T(8,128)(2,1)S(1)}, bf16[512,256]{1,0:T(8,128)(2,1)}, u32[]{:S(2)}) copy-start(bf16[512,256]{1,0:T(8,128)(2,1)} %get-tuple-element.72.rest_5_) | copy-start | bytes 786436 | tf_op jit(solution)/shard_map/cond
  40.3 1.5 %collective-permute-start.3 = (f32[64,512]{1,0:T(8,128)S(1)}, f32[64,512]{1,0:T(8,128)S(1)}, u32[]{:S(2)}, u32[]{:S(2)}) collective-permute-start(f32[64,512]{1,0:T(8,128)S(1)} %branch_1_fun.9), channel_id=1, source_target_pairs={{1,0},{0,1},{3,2},{2,3},{5,4},{4,5},{7,6},{6,7},{9,8},{8,9},{11,10... | collective-permute-start | bytes 393224 | tf_op jit(solution)/shard_map/cond/branch_1_fun/ppermute | solution.py:367
  41.9 7.6 %collective-permute-start.5 = (f32[64,512]{1,0:T(8,128)S(1)}, f32[64,512]{1,0:T(8,128)S(1)}, u32[]{:S(2)}, u32[]{:S(2)}) collective-permute-start(f32[64,512]{1,0:T(8,128)S(1)} %add.12.rest_0_), channel_id=1, source_target_pairs={{2,0},{3,1},{0,2},{1,3},{6,4},{7,5},{4,6},{5,7},{10,8},{11,9},{8,1... | collective-permute-start | bytes 393224 | tf_op jit(solution)/shard_map/cond/branch_1_fun/ppermute | solution.py:367
  48.6 1.0 %copy-start.10 = (bf16[512,256]{1,0:T(8,128)(2,1)S(1)}, bf16[512,256]{1,0:T(8,128)(2,1)}, u32[]{:S(2)}) copy-start(bf16[512,256]{1,0:T(8,128)(2,1)} %copy-done.9) | copy-start | bytes 786436 | tf_op jit(solution)/shard_map/cond
  51.0 1.3 %copy-start.4 = (bf16[512,2048]{1,0:T(8,128)(2,1)}, bf16[512,2048]{1,0:T(8,128)(2,1)S(1)}, u32[]{:S(2)}) copy-start(bf16[512,2048]{1,0:T(8,128)(2,1)S(1)} %get-tuple-element.115) | copy-start | bytes 6291460
  52.3 10.2 %collective-permute-start.16 = (bf16[512,256]{1,0:T(8,128)(2,1)}, bf16[512,256]{1,0:T(8,128)(2,1)S(1)}, u32[]{:S(2)}, u32[]{:S(2)}) collective-permute-start(bf16[512,256]{1,0:T(8,128)(2,1)} %get-tuple-element.149), channel_id=1, source_target_pairs={{2,0},{3,1},{0,2},{1,3},{6,4},{7,5},{4,6},{5,7},{10,8},{11,9},{8,1... | collective-permute-start | bytes 786440 | tf_op jit(solution)/shard_map/ppermute | solution.py:367
  52.8 9.7 %all-to-all-start = ((bf16[4,64,256]{2,1,0:T(8,128)(2,1)}), bf16[4,64,256]{2,1,0:T(8,128)(2,1)S(1)}, u32[]{:S(2)}, u32[]{:S(2)}) async-start(bf16[4,64,256]{2,1,0:T(8,128)(2,1)} %get-tuple-element.138), calls=%async_computation | async-start | bytes 262144 | tf_op jit(solution)/shard_map/all_to_all | solution.py:546
  56.5 6.1 %copy-start = (bf16[4,256,64]{1,2,0:T(8,128)(2,1)S(1)}, bf16[4,256,64]{1,2,0:T(8,128)(2,1)}, u32[]{:S(2)}) copy-start(bf16[4,256,64]{1,2,0:T(8,128)(2,1)} %param.25) | copy-start | bytes 393220
  56.5 6.1 %copy-start.1 = (f32[4,256,64]{1,2,0:T(8,128)S(1)}, f32[4,256,64]{1,2,0:T(8,128)}, u32[]{:S(2)}) copy-start(f32[4,256,64]{1,2,0:T(8,128)} %param.29) | copy-start | bytes 786436
  56.5 6.0 %copy-start.2 = (f32[4,256,64]{1,2,0:T(8,128)S(1)}, f32[4,256,64]{1,2,0:T(8,128)}, u32[]{:S(2)}) copy-start(f32[4,256,64]{1,2,0:T(8,128)} %param.30) | copy-start | bytes 786436
  56.5 6.0 %copy-start.3 = (f32[4,256,64]{1,2,0:T(8,128)S(1)}, f32[4,256,64]{1,2,0:T(8,128)}, u32[]{:S(2)}) copy-start(f32[4,256,64]{1,2,0:T(8,128)} %param.31) | copy-start | bytes 786436
where the time goes:
time: 65.1 us; the launch traced here: 64.7 us
  starting transfers between devices  27.7 us (43%)
  Pallas kernels  26.5 us (41%)
  waiting for transfers between devices  5.42 us (8%)
  local copies, waits for them, and re-layouts  2.7 us (4%)
  between operations  1.45 us (2%)
  other arithmetic  0.85 us (1%)
    ppermute x6, starting transfers between devices, fetch(): lax.ppermute(block, 'tok', [((i + slot) % tok_size, i) for i in range(tok...  12 us
    ppermute x8, starting transfers between devices, swap(): return lax.ppermute(block, axes, route)  6.32 us
    ppermute x3, starting transfers between devices, give_back(): lax.ppermute(block, 'tok', [((i - slot) % tok_size, i) for i in range(tok...  5.74 us
    pallas_call x1, Pallas kernels, adam_down(): pl.pallas_call(functools.partial(adam_kernel, slots), out_shape=shapes, i...  5.73 us
    pallas_call x1, Pallas kernels, input_whole(): pl.pallas_call(functools.partial(input_kernel, slots, narrow), grid=(wide...  5.11 us
    all_to_all x1, starting transfers between devices, per_device(): lax.all_to_all(part_up, 'tok', split_axis=0, concat_axis=0, tiled=True)  3.64 us
    ppermute x8, waiting for transfers between devices, swap(): return lax.ppermute(block, axes, route)  3.48 us
    pallas_call x1, Pallas kernels, per_device(): pl.pallas_call(functools.partial(select_kernel, slots, owned, tok_size),...  3.1 us
  transfers between devices with their start and end apart: 18, of which 5 were waited for; matrix products, arithmetic and copies ran while one was open for 3% of the time, Pallas kernels for 33%

commit v1 on v0

--- a/solution.py
+++ b/solution.py
@@ -210,11 +210,8 @@
 def each_rows(count, body):
     rows = 16
 
-    def step(i, _):
-        body(pl.ds(pl.multiple_of(i * rows, rows), rows), rows)
-        return 0
-
-    lax.fori_loop(0, count // rows, step, 0)
+    for i in range(count // rows):
+        body(slice(i * rows, (i + 1) * rows), rows)
 
 
 def adam_kernel(slots, facts, *rest):

time: 65.1 us -> 64.8 us (level)
  no operation moved by 1% of the time
where the time goes in v1:
time: 64.8 us; the launch traced here: 64.4 us
  starting transfers between devices  27.7 us (43%)
  Pallas kernels  26.3 us (41%)
  waiting for transfers between devices  5.32 us (8%)
  local copies, waits for them, and re-layouts  2.7 us (4%)
  between operations  1.45 us (2%)
  other arithmetic  0.85 us (1%)
    ppermute x6, starting transfers between devices, fetch(): lax.ppermute(block, 'tok', [((i + slot) % tok_size, i) for i in range(tok...  12 us
    ppermute x8, starting transfers between devices, swap(): return lax.ppermute(block, axes, route)  6.32 us
    pallas_call x1, Pallas kernels, adam_down(): pl.pallas_call(functools.partial(adam_kernel, slots), out_shape=shapes, i...  5.83 us
    ppermute x3, starting transfers between devices, give_back(): lax.ppermute(block, 'tok', [((i - slot) % tok_size, i) for i in range(tok...  5.74 us
    pallas_call x1, Pallas kernels, input_whole(): pl.pallas_call(functools.partial(input_kernel, slots, narrow), grid=(wide...  5.11 us
    all_to_all x1, starting transfers between devices, per_device(): lax.all_to_all(part_up, 'tok', split_axis=0, concat_axis=0, tiled=True)  3.64 us
    ppermute x8, waiting for transfers between devices, swap(): return lax.ppermute(block, axes, route)  3.48 us
    pallas_call x1, Pallas kernels, per_device(): pl.pallas_call(functools.partial(select_kernel, slots, owned, tok_size),...  3.1 us
  transfers between devices with their start and end apart: 18, of which 5 were waited for; matrix products, arithmetic and copies ran while one was open for 3% of the time, Pallas kernels for 33%

profile of v1, /device:TPU:0, one launch (start us, length us, event | category | flops | bytes accessed | tf_op | source)
XLA Modules:
  0.0 64.4 jit_solution(1175805401425608409)
XLA Ops:
  0.6 3.1 %shard_map.181 = (s32[8]{0:T(128)S(1)}, bf16[64,256]{1,0:T(8,128)(2,1)S(1)}, bf16[64,256]{1,0:T(8,128)(2,1)}, bf16[64,256]{1,0:T(8,128)(2,1)}, bf16[64,256]{1,0:...) custom-call(s32[4,4]{1,0:T(4,128)} %counts.1, ...), custom_call_target="tpu_custom_call" | custom-call | bytes 7077888 | tf_op jit(solution)/shard_map/pallas_call | solution.py:413
  3.7 5.1 %collective-permute-start.6 = (bf16[64,2048]{1,0:T(8,128)(2,1)}, bf16[64,2048]{1,0:T(8,128)(2,1)S(1)}, u32[]{:S(2)}, u32[]{:S(2)}) collective-permute-start(bf16[64,2048]{1,0:T(8,128)(2,1)} %get-tuple-element.122), channel_id=1, source_target_pairs={{4,0},{8,4},{12,8},{0,12},{5,1},{9,5},{13,9},{1,13},{6,2},{10,6},{... | collective-permute-start | bytes 786440 | tf_op jit(solution)/shard_map/ppermute | solution.py:400
  8.8 1.5 %collective-permute-start.9 = (bf16[512,256]{1,0:T(8,128)(2,1)}, bf16[512,256]{1,0:T(8,128)(2,1)S(1)}, u32[]{:S(2)}, u32[]{:S(2)}) collective-permute-start(bf16[512,256]{1,0:T(8,128)(2,1)} %own.1), channel_id=1, source_target_pairs={{2,0},{3,1},{0,2},{1,3},{6,4},{7,5},{4,6},{5,7},{10,8},{11,9},{8,1... | collective-permute-start | bytes 786440 | tf_op jit(solution)/shard_map/ppermute | solution.py:364
  10.3 0.4 collective-permute-start.10
  10.8 0.0 collective-permute-start.11
  10.8 1.6 %collective-permute-start.12 = (bf16[64,256]{1,0:T(8,128)(2,1)}, bf16[64,256]{1,0:T(8,128)(2,1)S(1)}, u32[]{:S(2)}, u32[]{:S(2)}) collective-permute-start(bf16[64,256]{1,0:T(8,128)(2,1)} %get-tuple-element.133), channel_id=1, source_target_pairs={{12,0},{0,4},{4,8},{8,12},{13,1},{1,5},{5,9},{9,13},{14,2},{2,6},{... | collective-permute-start | bytes 98312 | tf_op jit(solution)/shard_map/ppermute | solution.py:400
  12.4 1.2 %slice.15 = s32[1,1]{1,0:T(1,128)} slice(s32[4,4]{1,0:T(4,128)} %counts.1), slice={[0:1], [0:1]} | slice | bytes 8 | tf_op jit(solution)/shard_map/slice | solution.py:425
  14.2 1.7 %collective-permute-done.6 = bf16[64,2048]{1,0:T(8,128)(2,1)S(1)} collective-permute-done((bf16[64,2048]{1,0:T(8,128)(2,1)}, bf16[64,2048]{1,0:T(8,128)(2,1)S(1)}, u32[]{:S(2)}, u32[]{:S(2)}) %collective-permute-start.6) | collective-permute-done | bytes 262176 | tf_op jit(solution)/shard_map/ppermute | solution.py:400
  15.9 1.4 %collective-permute-start.7 = (bf16[64,2048]{1,0:T(8,128)(2,1)}, bf16[64,2048]{1,0:T(8,128)(2,1)}, u32[]{:S(2)}, u32[]{:S(2)}) collective-permute-start(bf16[64,2048]{1,0:T(8,128)(2,1)} %get-tuple-element.124), channel_id=1, source_target_pairs={{8,0},{12,4},{0,8},{4,12},{9,1},{13,5},{1,9},{5,13},{10,2},{14,6},... | collective-permute-start | bytes 786440 | tf_op jit(solution)/shard_map/ppermute | solution.py:400
  17.3 3.5 %collective-permute-start.8 = (bf16[64,2048]{1,0:T(8,128)(2,1)}, bf16[64,2048]{1,0:T(8,128)(2,1)}, u32[]{:S(2)}, u32[]{:S(2)}) collective-permute-start(bf16[64,2048]{1,0:T(8,128)(2,1)} %get-tuple-element.126), channel_id=1, source_target_pairs={{12,0},{0,4},{4,8},{8,12},{13,1},{1,5},{5,9},{9,13},{14,2},{2,6},{... | collective-permute-start | bytes 786440 | tf_op jit(solution)/shard_map/ppermute | solution.py:400
  20.7 1.0 %shard_map.182 = bf16[2,512,256]{2,1,0:T(8,128)(2,1)S(1)} custom-call(bf16[512,256]{1,0:T(8,128)(2,1)} %own.1, bf16[512,256]{1,0:T(8,128)(2,1)S(1)} %collective-permute-done.9.across), custom_call_target="tpu_custom_call" | custom-call | flops 6442450944 | bytes 50331648 | tf_op jit(solution)/shard_map/pallas_call | solution.py:301
  21.7 0.0 collective-permute-done.10.rest_6_
  21.8 0.0 collective-permute-done.12.rest_8_
  21.8 10.0 %conditional.2 = (bf16[2,512,256]{2,1,0:T(8,128)(2,1)}, f32[2,512,256]{2,1,0:T(8,128)S(1)}, f32[2,512,256]{2,1,0:T(8,128)S(1)}, bf16[256,512]{1,0:T(8,128)(2,1)S...) conditional(s32[]{:T(128)} %convert_element_type.10, () %tuple.39, ...), branch_computations={%region_0.0_spmd, %region_1.0_spmd} | conditional | flops 8254423040 | bytes 29491384 | solution.py:440
  21.8 0.8 %branch_1_fun.6 = f32[64,512]{1,0:T(8,128)S(1)} custom-call(s32[8]{0:T(128)S(1)} %get-tuple-element.47.facts, bf16[512,256]{1,0:T(8,128)(2,1)S(1)} %get-tuple-element.48.grad, bf16[64,256]{1,0:T(8,128)(2,1)S(1)} %get-tuple-element.49.rest_0_, bf16[64,256]{1,0:T(8,128)(2,1)S(1)} %get-tuple-element.50.rest_1_, bf16[64,256]{1,0:T(8,128)(2,1)S(1)} %get-tuple-element.51.rest_2_, ...), custom_call_target="tpu_custom_call" | custom-call | flops 201326592 | bytes 786432 | tf_op jit(solution)/shard_map/cond/branch_1_fun/pallas_call | solution.py:443
  22.6 0.1 collective-permute-start.1
  22.7 0.5 collective-permute-start
  23.2 0.8 %collective-permute-done.1 = f32[64,512]{1,0:T(8,128)S(1)} collective-permute-done((f32[64,512]{1,0:T(8,128)S(1)}, f32[64,512]{1,0:T(8,128)S(1)}, u32[]{:S(2)}, u32[]{:S(2)}) %collective-permute-start.1) | collective-permute-done | bytes 131104 | tf_op jit(solution)/shard_map/cond/branch_1_fun/ppermute | solution.py:364
  24.1 1.6 %collective-permute-start.2 = (f32[64,512]{1,0:T(8,128)S(1)}, f32[64,512]{1,0:T(8,128)S(1)}, u32[]{:S(2)}, u32[]{:S(2)}) collective-permute-start(f32[64,512]{1,0:T(8,128)S(1)} %add.11.rest_0_), channel_id=1, source_target_pairs={{2,0},{3,1},{0,2},{1,3},{6,4},{7,5},{4,6},{5,7},{10,8},{11,9},{8,1... | collective-permute-start | bytes 393224 | tf_op jit(solution)/shard_map/cond/branch_1_fun/ppermute | solution.py:364
  25.7 2.4 %branch_1_fun.7 = (f32[2,512,256]{2,1,0:T(8,128)S(1)}, f32[2,512,256]{2,1,0:T(8,128)S(1)}) custom-call(bf16[512,2048]{1,0:T(8,128)(2,1)S(1)} %get-tuple-element.45.tokens, bf16[2048,1024]{1,0:T(8,128)(2,1)S(1)} %get-tuple-element.53.weight), custom_call_target="tpu_custom_call" | custom-call | flops 6442450944 | bytes 18874368 | tf_op jit(solution)/shard_map/cond/branch_1_fun/pallas_call | solution.py:453
  28.0 1.6 %collective-permute-done.2.rest_1_ = f32[64,512]{1,0:T(8,128)S(1)} collective-permute-done((f32[64,512]{1,0:T(8,128)S(1)}, f32[64,512]{1,0:T(8,128)S(1)}, u32[]{:S(2)}, u32[]{:S(2)}) %collective-permute-start.2) | collective-permute-done | bytes 131104 | tf_op jit(solution)/shard_map/cond/branch_1_fun/ppermute | solution.py:364
  29.7 2.1 %branch_1_fun.8 = (bf16[256,512]{1,0:T(8,128)(2,1)S(1)}, bf16[64,2048]{1,0:T(8,128)(2,1)S(1)}, bf16[64,2048]{1,0:T(8,128)(2,1)}, bf16[64,2048]{1,0:T(8,128)(2,1)}, bf16[64,2048]{1,0:T(8,128)(2,1)}) custom-call(s32[8]{0:T(128)S(1)} %get-tuple-element.47.facts, bf16[512,2048]{1,0:T(8,128)(2,1)S(1)} %get-tuple-element.45.tokens, f32[64,512]{1,0:T(8,128)S(1)} %add.11.rest_0_, ...), custom_call_target="tpu_custom_call" | custom-call | flops 1610612736 | bytes 6291456 | tf_op jit(solution)/shard_map/cond/branch_1_fun/pallas_call | solution.py:466
  31.8 0.0 collective-permute-done
  31.8 3.7 %collective-permute-start.14 = (bf16[64,2048]{1,0:T(8,128)(2,1)}, bf16[64,2048]{1,0:T(8,128)(2,1)}, u32[]{:S(2)}, u32[]{:S(2)}) collective-permute-start(bf16[64,2048]{1,0:T(8,128)(2,1)} %get-tuple-element.142), channel_id=1, source_target_pairs={{8,0},{12,4},{0,8},{4,12},{9,1},{13,5},{1,9},{5,13},{10,2},{14,6},... | collective-permute-start | bytes 786440 | tf_op jit(solution)/shard_map/ppermute | solution.py:403
  35.5 0.2 collective-permute-start.15
  35.7 1.8 %collective-permute-start.13 = (bf16[64,2048]{1,0:T(8,128)(2,1)}, bf16[64,2048]{1,0:T(8,128)(2,1)}, u32[]{:S(2)}, u32[]{:S(2)}) collective-permute-start(bf16[64,2048]{1,0:T(8,128)(2,1)} %get-tuple-element.141), channel_id=1, source_target_pairs={{12,0},{0,4},{4,8},{8,12},{13,1},{1,5},{5,9},{9,13},{14,2},{2,6},{... | collective-permute-start | bytes 786440 | tf_op jit(solution)/shard_map/ppermute | solution.py:403
  37.6 13.5 %conditional.3 = (bf16[256,512]{1,0:T(8,128)(2,1)S(1)}, bf16[4,64,256]{2,1,0:T(8,128)(2,1)}, f32[512,256]{1,0:T(8,128)S(1)}, bf16[512,256]{1,0:T(8,128)(2,1)}, bf16[512,2048]{1,0:T(8,128)(2,1)S(1)}) conditional(s32[]{:T(128)} %convert_element_type.10, () %tuple.36, (s32[8]{0:T(128)S(1)}, bf16[512,2048]{1,0:T(8,128)(2,1)}, bf16[64,2048]{1,0:T(8,128)(2,1)}, ...), branch_computations={%region_2.0_spmd, %region_3.0_spmd} | conditional | flops 9865428992 | bytes 56492360 | solution.py:440
  37.6 0.0 copy-start.13
  37.6 0.0 copy-start.15
  37.6 2.7 %branch_1_fun.9 = f32[64,512]{1,0:T(8,128)S(1)} custom-call(s32[8]{0:T(128)S(1)} %get-tuple-element.62.facts, bf16[512,2048]{1,0:T(8,128)(2,1)} %get-tuple-element.64.tokens, bf16[64,2048]{1,0:T(8,128)(2,1)} %get-tuple-element.65.rest_0_, bf16[64,2048]{1,0:T(8,128)(2,1)} %get-tuple-element.66.rest_1_, bf16[64,2048]{1,0:T(8,128)(2,1)} %get-tuple-element.67.rest_2_, ...), custom_call_target="tpu_custom_call" | custom-call | flops 1610612736 | bytes 6291456 | tf_op jit(solution)/shard_map/cond/branch_1_fun/pallas_call | solution.py:510
  40.3 0.6 collective-permute-start.3
  40.9 1.0 %collective-permute-done.3 = f32[64,512]{1,0:T(8,128)S(1)} collective-permute-done((f32[64,512]{1,0:T(8,128)S(1)}, f32[64,512]{1,0:T(8,128)S(1)}, u32[]{:S(2)}, u32[]{:S(2)}) %collective-permute-start.3) | collective-permute-done | bytes 131104 | tf_op jit(solution)/shard_map/cond/branch_1_fun/ppermute | solution.py:364
  41.9 1.6 %collective-permute-start.5 = (f32[64,512]{1,0:T(8,128)S(1)}, f32[64,512]{1,0:T(8,128)S(1)}, u32[]{:S(2)}, u32[]{:S(2)}) collective-permute-start(f32[64,512]{1,0:T(8,128)S(1)} %add.12.rest_0_), channel_id=1, source_target_pairs={{2,0},{3,1},{0,2},{1,3},{6,4},{7,5},{4,6},{5,7},{10,8},{11,9},{8,1... | collective-permute-start | bytes 393224 | tf_op jit(solution)/shard_map/cond/branch_1_fun/ppermute | solution.py:364
  43.5 5.1 %branch_1_fun.10 = bf16[512,2048]{1,0:T(8,128)(2,1)S(1)} custom-call(bf16[256,512]{1,0:T(8,128)(2,1)S(1)} %get-tuple-element.70.spread, bf16[2048,1024]{1,0:T(8,128)(2,1)S(1)} %copy-done.6, bf16[64,2048]{1,0:T(8,128)(2,1)S(1)} %copy-done.11, bf16[64,2048]{1,0:T(8,128)(2,1)S(1)} %copy-done.13, bf16[64,2048]{1,0:T(8,128)(2,1)} %get-tuple-element.67.rest_2_, ...), custom_call_target="tpu_custom_call" | custom-call | flops 8053063680 | bytes 18874368 | tf_op jit(solution)/shard_map/cond/branch_1_fun/pallas_call | solution.py:488
  48.6 0.0 copy-start.10
  48.6 0.8 %fusion.2 = (bf16[512,256]{1,0:T(8,128)(2,1)}, f32[512,256]{1,0:T(8,128)S(1)}) fusion(f32[2,512,256]{2,1,0:T(8,128)S(1)} %collective-permute-done.4, f32[2,512,256]{2,1,0:T(8,128)S(1)} %get-tuple-element.74), kind=kLoop, calls=%fused_computation.4 | loop fusion | flops 393216 | bytes 2883584 | tf_op jit(solution)/shard_map/cond/branch_1_fun/convert_element_type | solution.py:523
  49.5 0.1 copy-done.10
  49.6 1.4 %branch_1_fun.11 = (bf16[256,512]{1,0:T(8,128)(2,1)S(1)}, bf16[4,64,256]{2,1,0:T(8,128)(2,1)}) custom-call(s32[8]{0:T(128)S(1)} %get-tuple-element.62.facts, bf16[512,256]{1,0:T(8,128)(2,1)S(1)} %copy-done.10, f32[64,512]{1,0:T(8,128)S(1)} %add.12.rest_0_, f32[64,512]{1,0:T(8,128)S(1)} %collective-permute-done.5.rest_1_), custom_call_target="tpu_custom_call" | custom-call | flops 201326592 | bytes 786432 | tf_op jit(solution)/shard_map/cond/branch_1_fun/pallas_call | solution.py:529
  51.0 1.3 %copy-done.4 = bf16[512,2048]{1,0:T(8,128)(2,1)} copy-done((bf16[512,2048]{1,0:T(8,128)(2,1)}, bf16[512,2048]{1,0:T(8,128)(2,1)S(1)}, u32[]{:S(2)}) %copy-start.4) | copy-done | bytes 2097176
  52.3 0.5 collective-permute-start.16
  52.8 3.6 %all-to-all-start = ((bf16[4,64,256]{2,1,0:T(8,128)(2,1)}), bf16[4,64,256]{2,1,0:T(8,128)(2,1)S(1)}, u32[]{:S(2)}, u32[]{:S(2)}) async-start(bf16[4,64,256]{2,1,0:T(8,128)(2,1)} %get-tuple-element.138), calls=%async_computation | async-start | bytes 262144 | tf_op jit(solution)/shard_map/all_to_all | solution.py:543
  56.5 0.0 copy-start
  56.5 0.0 copy-start.1
  56.5 0.0 copy-start.2
  56.5 0.0 copy-start.3
  56.5 5.8 %shard_map.183 = (bf16[4,64,2048]{2,1,0:T(8,128)(2,1)}, f32[4,64,2048]{2,1,0:T(8,128)}) custom-call(s32[8]{0:T(128)S(1)} %get-tuple-element.120.facts, bf16[64,2048]{1,0:T(8,128)(2,1)S(1)} %get-tuple-element.139.rest_0_, bf16[64,2048]{1,0:T(8,128)(2,1)} %collective-permute-done.13.rest_1_, bf16[64,2048]{1,0:T(8,128)(2,1)} %collective-permute-done.14.rest_2_, ...), custom_call_target="tpu_custom_call" | custom-call | flops 31457280 | bytes 94371840 | tf_op jit(solution)/shard_map/pallas_call | solution.py:276
  62.4 0.2 all-to-all-done.came
  62.6 1.9 %shard_map.184 = (bf16[4,64,256]{2,1,0:T(8,128)(2,1)}, f32[4,64,256]{2,1,0:T(8,128)}, bf16[512,256]{1,0:T(8,128)(2,1)}) custom-call(s32[8]{0:T(128)S(1)} %get-tuple-element.120.facts, bf16[4,64,256]{2,1,0:T(8,128)(2,1)S(1)} %all-to-all-done.came, bf16[4,64,256]{2,1,0:T(8,128)(2,1)S(1)} %bitcast.18, f32[4,64,256]{2,1,0:T(8,128)S(1)} %bitcast.19, ...), custom_call_target="tpu_custom_call" | custom-call | flops 3932160 | bytes 3932160 | tf_op jit(solution)/shard_map/pallas_call | solution.py:338
  (36 shorter events, 0.1 us)
Async XLA Ops:
  3.7 12.1 %collective-permute-start.6 = (bf16[64,2048]{1,0:T(8,128)(2,1)}, bf16[64,2048]{1,0:T(8,128)(2,1)S(1)}, u32[]{:S(2)}, u32[]{:S(2)}) collective-permute-start(bf16[64,2048]{1,0:T(8,128)(2,1)} %get-tuple-element.122), channel_id=1, source_target_pairs={{4,0},{8,4},{12,8},{0,12},{5,1},{9,5},{13,9},{1,13},{6,2},{10,6},{... | collective-permute-start | bytes 786440 | tf_op jit(solution)/shard_map/ppermute | solution.py:400
  8.8 8.4 %collective-permute-start.9 = (bf16[512,256]{1,0:T(8,128)(2,1)}, bf16[512,256]{1,0:T(8,128)(2,1)S(1)}, u32[]{:S(2)}, u32[]{:S(2)}) collective-permute-start(bf16[512,256]{1,0:T(8,128)(2,1)} %own.1), channel_id=1, source_target_pairs={{2,0},{3,1},{0,2},{1,3},{6,4},{7,5},{4,6},{5,7},{10,8},{11,9},{8,1... | collective-permute-start | bytes 786440 | tf_op jit(solution)/shard_map/ppermute | solution.py:364
  10.3 11.4 %collective-permute-start.10 = (bf16[64,256]{1,0:T(8,128)(2,1)}, bf16[64,256]{1,0:T(8,128)(2,1)S(1)}, u32[]{:S(2)}, u32[]{:S(2)}) collective-permute-start(bf16[64,256]{1,0:T(8,128)(2,1)} %get-tuple-element.131), channel_id=1, source_target_pairs={{4,0},{8,4},{12,8},{0,12},{5,1},{9,5},{13,9},{1,13},{6,2},{10,6},{... | collective-permute-start | bytes 98312 | tf_op jit(solution)/shard_map/ppermute | solution.py:400
  10.8 11.0 %collective-permute-start.11 = (bf16[64,256]{1,0:T(8,128)(2,1)}, bf16[64,256]{1,0:T(8,128)(2,1)S(1)}, u32[]{:S(2)}, u32[]{:S(2)}) collective-permute-start(bf16[64,256]{1,0:T(8,128)(2,1)} %get-tuple-element.132), channel_id=1, source_target_pairs={{8,0},{12,4},{0,8},{4,12},{9,1},{13,5},{1,9},{5,13},{10,2},{14,6},... | collective-permute-start | bytes 98312 | tf_op jit(solution)/shard_map/ppermute | solution.py:400
  10.8 11.0 %collective-permute-start.12 = (bf16[64,256]{1,0:T(8,128)(2,1)}, bf16[64,256]{1,0:T(8,128)(2,1)S(1)}, u32[]{:S(2)}, u32[]{:S(2)}) collective-permute-start(bf16[64,256]{1,0:T(8,128)(2,1)} %get-tuple-element.133), channel_id=1, source_target_pairs={{12,0},{0,4},{4,8},{8,12},{13,1},{1,5},{5,9},{9,13},{14,2},{2,6},{... | collective-permute-start | bytes 98312 | tf_op jit(solution)/shard_map/ppermute | solution.py:400
  15.9 5.9 %copy-start.12 = (bf16[64,2048]{1,0:T(8,128)(2,1)}, bf16[64,2048]{1,0:T(8,128)(2,1)S(1)}, u32[]{:S(2)}) copy-start(bf16[64,2048]{1,0:T(8,128)(2,1)S(1)} %collective-permute-done.6) | copy-start | bytes 786436
  15.9 5.9 %copy-start.5 = (bf16[2048,1024]{1,0:T(8,128)(2,1)S(1)}, bf16[2048,1024]{1,0:T(8,128)(2,1)}, u32[]{:S(2)}) copy-start(bf16[2048,1024]{1,0:T(8,128)(2,1)} %param.19) | copy-start | bytes 12582916
  15.9 5.9 %copy-start.7 = (bf16[512,2048]{1,0:T(8,128)(2,1)S(1)}, bf16[512,2048]{1,0:T(8,128)(2,1)}, u32[]{:S(2)}) copy-start(bf16[512,2048]{1,0:T(8,128)(2,1)} %param.18) | copy-start | bytes 6291460
  15.9 5.9 %copy-start.8 = (bf16[512,256]{1,0:T(8,128)(2,1)S(1)}, bf16[512,256]{1,0:T(8,128)(2,1)}, u32[]{:S(2)}) copy-start(bf16[512,256]{1,0:T(8,128)(2,1)} %own.1) | copy-start | bytes 786436
  15.9 19.6 %collective-permute-start.7 = (bf16[64,2048]{1,0:T(8,128)(2,1)}, bf16[64,2048]{1,0:T(8,128)(2,1)}, u32[]{:S(2)}, u32[]{:S(2)}) collective-permute-start(bf16[64,2048]{1,0:T(8,128)(2,1)} %get-tuple-element.124), channel_id=1, source_target_pairs={{8,0},{12,4},{0,8},{4,12},{9,1},{13,5},{1,9},{5,13},{10,2},{14,6},... | collective-permute-start | bytes 786440 | tf_op jit(solution)/shard_map/ppermute | solution.py:400
  17.3 4.5 %copy-start.14 = (bf16[512,256]{1,0:T(8,128)(2,1)}, bf16[512,256]{1,0:T(8,128)(2,1)S(1)}, u32[]{:S(2)}) copy-start(bf16[512,256]{1,0:T(8,128)(2,1)S(1)} %collective-permute-done.9.across) | copy-start | bytes 786436
  17.3 18.3 %collective-permute-start.8 = (bf16[64,2048]{1,0:T(8,128)(2,1)}, bf16[64,2048]{1,0:T(8,128)(2,1)}, u32[]{:S(2)}, u32[]{:S(2)}) collective-permute-start(bf16[64,2048]{1,0:T(8,128)(2,1)} %get-tuple-element.126), channel_id=1, source_target_pairs={{12,0},{0,4},{4,8},{8,12},{13,1},{1,5},{5,9},{9,13},{14,2},{2,6},{... | collective-permute-start | bytes 786440 | tf_op jit(solution)/shard_map/ppermute | solution.py:400
  22.6 1.4 %collective-permute-start.1 = (f32[64,512]{1,0:T(8,128)S(1)}, f32[64,512]{1,0:T(8,128)S(1)}, u32[]{:S(2)}, u32[]{:S(2)}) collective-permute-start(f32[64,512]{1,0:T(8,128)S(1)} %branch_1_fun.6), channel_id=1, source_target_pairs={{1,0},{0,1},{3,2},{2,3},{5,4},{4,5},{7,6},{6,7},{9,8},{8,9},{11,10... | collective-permute-start | bytes 393224 | tf_op jit(solution)/shard_map/cond/branch_1_fun/ppermute | solution.py:364
  22.7 9.1 %collective-permute-start = (bf16[2,512,256]{2,1,0:T(8,128)(2,1)S(1)}, bf16[2,512,256]{2,1,0:T(8,128)(2,1)}, u32[]{:S(2)}, u32[]{:S(2)}) collective-permute-start(bf16[2,512,256]{2,1,0:T(8,128)(2,1)S(1)} %get-tuple-element.44), channel_id=1, source_target_pairs={{1,0},{0,1},{3,2},{2,3},{5,4},{4,5},{7,6},{6,7},{9,8},{8,9},{11,10... | collective-permute-start | bytes 1572872 | tf_op jit(solution)/shard_map/cond/branch_1_fun/ppermute | solution.py:364
  24.1 5.6 %collective-permute-start.2 = (f32[64,512]{1,0:T(8,128)S(1)}, f32[64,512]{1,0:T(8,128)S(1)}, u32[]{:S(2)}, u32[]{:S(2)}) collective-permute-start(f32[64,512]{1,0:T(8,128)S(1)} %add.11.rest_0_), channel_id=1, source_target_pairs={{2,0},{3,1},{0,2},{1,3},{6,4},{7,5},{4,6},{5,7},{10,8},{11,9},{8,1... | collective-permute-start | bytes 393224 | tf_op jit(solution)/shard_map/cond/branch_1_fun/ppermute | solution.py:364
  31.8 24.7 %collective-permute-start.14 = (bf16[64,2048]{1,0:T(8,128)(2,1)}, bf16[64,2048]{1,0:T(8,128)(2,1)}, u32[]{:S(2)}, u32[]{:S(2)}) collective-permute-start(bf16[64,2048]{1,0:T(8,128)(2,1)} %get-tuple-element.142), channel_id=1, source_target_pairs={{8,0},{12,4},{0,8},{4,12},{9,1},{13,5},{1,9},{5,13},{10,2},{14,6},... | collective-permute-start | bytes 786440 | tf_op jit(solution)/shard_map/ppermute | solution.py:403
  35.5 21.0 %collective-permute-start.15 = (bf16[64,2048]{1,0:T(8,128)(2,1)}, bf16[64,2048]{1,0:T(8,128)(2,1)}, u32[]{:S(2)}, u32[]{:S(2)}) collective-permute-start(bf16[64,2048]{1,0:T(8,128)(2,1)} %get-tuple-element.144), channel_id=1, source_target_pairs={{4,0},{8,4},{12,8},{0,12},{5,1},{9,5},{13,9},{1,13},{6,2},{10,6},{... | collective-permute-start | bytes 786440 | tf_op jit(solution)/shard_map/ppermute | solution.py:403
  35.7 20.8 %collective-permute-start.13 = (bf16[64,2048]{1,0:T(8,128)(2,1)}, bf16[64,2048]{1,0:T(8,128)(2,1)}, u32[]{:S(2)}, u32[]{:S(2)}) collective-permute-start(bf16[64,2048]{1,0:T(8,128)(2,1)} %get-tuple-element.141), channel_id=1, source_target_pairs={{12,0},{0,4},{4,8},{8,12},{13,1},{1,5},{5,9},{9,13},{14,2},{2,6},{... | collective-permute-start | bytes 786440 | tf_op jit(solution)/shard_map/ppermute | solution.py:403
  37.6 5.9 %copy-start.9 = (bf16[512,256]{1,0:T(8,128)(2,1)}, bf16[512,256]{1,0:T(8,128)(2,1)S(1)}, u32[]{:S(2)}) copy-start(bf16[512,256]{1,0:T(8,128)(2,1)S(1)} %get-tuple-element.63.rest_4_.grad) | copy-start | bytes 786436 | tf_op jit(solution)/shard_map/cond
  37.6 11.1 %collective-permute-start.4 = (f32[2,512,256]{2,1,0:T(8,128)S(1)}, f32[2,512,256]{2,1,0:T(8,128)S(1)}, u32[]{:S(2)}, u32[]{:S(2)}) collective-permute-start(f32[2,512,256]{2,1,0:T(8,128)S(1)} %get-tuple-element.75), channel_id=1, source_target_pairs={{1,0},{0,1},{3,2},{2,3},{5,4},{4,5},{7,6},{6,7},{9,8},{8,9},{11,10... | collective-permute-start | bytes 3145736 | tf_op jit(solution)/shard_map/cond/branch_1_fun/ppermute | solution.py:364
  37.6 5.9 %copy-start.6 = (bf16[2048,1024]{1,0:T(8,128)(2,1)S(1)}, bf16[2048,1024]{1,0:T(8,128)(2,1)}, u32[]{:S(2)}) copy-start(bf16[2048,1024]{1,0:T(8,128)(2,1)} %get-tuple-element.71.weight) | copy-start | bytes 12582916 | tf_op jit(solution)/shard_map/cond
  37.6 5.9 %copy-start.11 = (bf16[64,2048]{1,0:T(8,128)(2,1)S(1)}, bf16[64,2048]{1,0:T(8,128)(2,1)}, u32[]{:S(2)}) copy-start(bf16[64,2048]{1,0:T(8,128)(2,1)} %get-tuple-element.65.rest_0_) | copy-start | bytes 786436 | tf_op jit(solution)/shard_map/cond
  37.6 5.9 %copy-start.13 = (bf16[64,2048]{1,0:T(8,128)(2,1)S(1)}, bf16[64,2048]{1,0:T(8,128)(2,1)}, u32[]{:S(2)}) copy-start(bf16[64,2048]{1,0:T(8,128)(2,1)} %get-tuple-element.66.rest_1_) | copy-start | bytes 786436 | tf_op jit(solution)/shard_map/cond
  37.6 5.9 %copy-start.15 = (bf16[512,256]{1,0:T(8,128)(2,1)S(1)}, bf16[512,256]{1,0:T(8,128)(2,1)}, u32[]{:S(2)}) copy-start(bf16[512,256]{1,0:T(8,128)(2,1)} %get-tuple-element.72.rest_5_) | copy-start | bytes 786436 | tf_op jit(solution)/shard_map/cond
  40.3 1.5 %collective-permute-start.3 = (f32[64,512]{1,0:T(8,128)S(1)}, f32[64,512]{1,0:T(8,128)S(1)}, u32[]{:S(2)}, u32[]{:S(2)}) collective-permute-start(f32[64,512]{1,0:T(8,128)S(1)} %branch_1_fun.9), channel_id=1, source_target_pairs={{1,0},{0,1},{3,2},{2,3},{5,4},{4,5},{7,6},{6,7},{9,8},{8,9},{11,10... | collective-permute-start | bytes 393224 | tf_op jit(solution)/shard_map/cond/branch_1_fun/ppermute | solution.py:364
  41.9 7.6 %collective-permute-start.5 = (f32[64,512]{1,0:T(8,128)S(1)}, f32[64,512]{1,0:T(8,128)S(1)}, u32[]{:S(2)}, u32[]{:S(2)}) collective-permute-start(f32[64,512]{1,0:T(8,128)S(1)} %add.12.rest_0_), channel_id=1, source_target_pairs={{2,0},{3,1},{0,2},{1,3},{6,4},{7,5},{4,6},{5,7},{10,8},{11,9},{8,1... | collective-permute-start | bytes 393224 | tf_op jit(solution)/shard_map/cond/branch_1_fun/ppermute | solution.py:364
  48.6 1.0 %copy-start.10 = (bf16[512,256]{1,0:T(8,128)(2,1)S(1)}, bf16[512,256]{1,0:T(8,128)(2,1)}, u32[]{:S(2)}) copy-start(bf16[512,256]{1,0:T(8,128)(2,1)} %copy-done.9) | copy-start | bytes 786436 | tf_op jit(solution)/shard_map/cond
  51.0 1.3 %copy-start.4 = (bf16[512,2048]{1,0:T(8,128)(2,1)}, bf16[512,2048]{1,0:T(8,128)(2,1)S(1)}, u32[]{:S(2)}) copy-start(bf16[512,2048]{1,0:T(8,128)(2,1)S(1)} %get-tuple-element.115) | copy-start | bytes 6291460
  52.3 10.2 %collective-permute-start.16 = (bf16[512,256]{1,0:T(8,128)(2,1)}, bf16[512,256]{1,0:T(8,128)(2,1)S(1)}, u32[]{:S(2)}, u32[]{:S(2)}) collective-permute-start(bf16[512,256]{1,0:T(8,128)(2,1)} %get-tuple-element.149), channel_id=1, source_target_pairs={{2,0},{3,1},{0,2},{1,3},{6,4},{7,5},{4,6},{5,7},{10,8},{11,9},{8,1... | collective-permute-start | bytes 786440 | tf_op jit(solution)/shard_map/ppermute | solution.py:364
  52.8 9.7 %all-to-all-start = ((bf16[4,64,256]{2,1,0:T(8,128)(2,1)}), bf16[4,64,256]{2,1,0:T(8,128)(2,1)S(1)}, u32[]{:S(2)}, u32[]{:S(2)}) async-start(bf16[4,64,256]{2,1,0:T(8,128)(2,1)} %get-tuple-element.138), calls=%async_computation | async-start | bytes 262144 | tf_op jit(solution)/shard_map/all_to_all | solution.py:543
  56.5 6.1 %copy-start = (bf16[4,256,64]{1,2,0:T(8,128)(2,1)S(1)}, bf16[4,256,64]{1,2,0:T(8,128)(2,1)}, u32[]{:S(2)}) copy-start(bf16[4,256,64]{1,2,0:T(8,128)(2,1)} %param.25) | copy-start | bytes 393220
  56.5 6.1 %copy-start.1 = (f32[4,256,64]{1,2,0:T(8,128)S(1)}, f32[4,256,64]{1,2,0:T(8,128)}, u32[]{:S(2)}) copy-start(f32[4,256,64]{1,2,0:T(8,128)} %param.29) | copy-start | bytes 786436
  56.5 6.0 %copy-start.2 = (f32[4,256,64]{1,2,0:T(8,128)S(1)}, f32[4,256,64]{1,2,0:T(8,128)}, u32[]{:S(2)}) copy-start(f32[4,256,64]{1,2,0:T(8,128)} %param.30) | copy-start | bytes 786436
  56.5 6.0 %copy-start.3 = (f32[4,256,64]{1,2,0:T(8,128)S(1)}, f32[4,256,64]{1,2,0:T(8,128)}, u32[]{:S(2)}) copy-start(f32[4,256,64]{1,2,0:T(8,128)} %param.31) | copy-start | bytes 786436
